TPU v7x, 32 devices: a whole 2x2x4 slice. The times are simulated.
32 devices in a mesh: groups: 2 (over y), req: 4 (over z), mp: 4 (over x, core).
Axes of the slice: x: 2, y: 2, z: 4, core: 2. Of those that a mesh axis runs over, the one named last changes fastest.
Arguments:
- tokens: bfloat16 [3072, 4096], P(('groups', 'req'), 'mp'), parts along dimension 0, may hold values from -6 to 6
- lengths: int32 [8, 128], P(('groups', 'req')), parts along dimension 0, may hold values from 1 to 4, 384 in all within a row
- adapter_holder_index: int32 [1024, 1], P(('groups', 'req')), parts along dimension 0, may hold values from 0 to 3; in each aligned block of 128 rows (0 to 127, 128 to 255, ...) at most 33 rows name the same one
- adapter_place_index: int32 [1024], P(('groups', 'req')), parts along dimension 0, may hold values from 0 to 4
- value_weight: bfloat16 [4096, 1024], P(None, 'mp'), may hold values from -0.09375 to 0.09375
- adapter_down_weight: bfloat16 [4096, 20, 64], P('mp', 'req'), may hold values from -0.09375 to 0.09375
- adapter_up_weight: bfloat16 [20, 64, 1024], P('req', None, 'mp'), may hold values from -0.75 to 0.75
Outputs:
- values_out: bfloat16 [3072, 1024], P(('groups', 'req'), 'mp'), parts along dimension 0
There are 2 independent parts, one for each index of `groups`. A program takes and returns all parts, laid end to end along the dimension named above; an argument that names none is the same for every part. Nothing has to cross between parts.
Inputs may be any that keep to these rules, and one draw needn't show every extreme that they name: `adapter_holder_index`: in each aligned block of 128 rows (the prompts of one index of req) no value appears more than 33 times, a bound that some block reaches. `lengths`: each row sums to 384.
All inputs are finite; a program needn't handle non-finite values.
Results may differ from a plain program's by a relative error of at most 0.0043.
Values may be sent and summed in bfloat16 or wider, within the bound.
A program may use at most 64 MiB of HBM per device.

v0:
```python
import jax
import jax.numpy as jnp
from jax import lax
from jax.sharding import PartitionSpec as P

LMAX = 4
REQ_DEV = 128


def grouped_update(token_rows, slot_ids, down_factor_sets, up_sets, reduce_fn):
    count = token_rows.shape[0] * token_rows.shape[1]
    flat_rows = token_rows.reshape(count, token_rows.shape[2])
    flat_ids = slot_ids.reshape(count)
    held = down_factor_sets.shape[0]
    blocks = (count + 127) // 128 + held
    grouped = blocks * 128
    valid = flat_ids >= 0
    member = (flat_ids[:, None] == jnp.arange(held, dtype=jnp.int32)[None, :]).astype(jnp.int32)
    group_sizes = jnp.sum(member, axis=0)
    padded = (group_sizes + 127) // 128 * 128
    group_end = jnp.cumsum(padded)
    group_start = group_end - padded
    within = jnp.sum(jnp.cumsum(member, axis=0) * member, axis=1) - 1
    target = jnp.where(valid, jnp.sum(member * group_start[None, :], axis=1) + within, grouped)
    source = (
        jnp.zeros((grouped,), jnp.int32)
        .at[target]
        .set(jnp.arange(count, dtype=jnp.int32), mode="drop")
    )
    filled = jnp.zeros((grouped,), jnp.bool_).at[target].set(True, mode="drop")
    grouped_rows = jnp.where(filled[:, None], flat_rows[source], jnp.zeros((), jnp.bfloat16))
    grouped_rows = grouped_rows.reshape(blocks, 128, flat_rows.shape[1])
    block_first = jnp.arange(blocks, dtype=jnp.int32) * 128
    block_adapter = jnp.minimum(
        jnp.sum((block_first[:, None] >= group_end[None, :]).astype(jnp.int32), axis=1), held - 1
    )
    partial_value = jnp.einsum(
        "bkf,bfr->bkr",
        grouped_rows,
        down_factor_sets[block_adapter],
        preferred_element_type=jnp.float32,
    )
    reduced_rank_output = reduce_fn(partial_value).astype(jnp.bfloat16)
    term = jnp.einsum(
        "bkr,brc->bkc",
        reduced_rank_output,
        up_sets[block_adapter],
        preferred_element_type=jnp.float32,
    )
    term = term.astype(jnp.bfloat16).reshape(grouped, up_sets.shape[2])
    picked = jnp.where(
        valid[:, None], term[jnp.minimum(target, grouped - 1)], jnp.zeros((), jnp.bfloat16)
    )
    return picked.reshape(token_rows.shape[0], token_rows.shape[1], up_sets.shape[2])


def body(
    tokens,
    lengths,
    adapter_holder_index,
    adapter_place_index,
    value_weight,
    adapter_down_weight,
    adapter_up_weight,
):
    tok_rows = tokens.shape[0]
    peers = lax.axis_size("req")
    request_cap = max(2, REQ_DEV // peers + 1)
    slots = request_cap * LMAX
    lengths_row = lengths[0]
    prompt_ends = jnp.cumsum(lengths_row)
    prompt_starts = prompt_ends - lengths_row
    owners = adapter_holder_index[:, 0]
    request_index = jnp.arange(REQ_DEV, dtype=jnp.int32)
    earlier = (owners[None, :] == owners[:, None]) & (
        request_index[None, :] < request_index[:, None]
    )
    rank_among = jnp.sum(earlier.astype(jnp.int32), axis=1)
    matches = (owners[None, None, :] == jnp.arange(peers, dtype=jnp.int32)[:, None, None]) & (
        rank_among[None, None, :] == jnp.arange(request_cap, dtype=jnp.int32)[None, :, None]
    )
    present = jnp.any(matches, axis=2)
    chosen = jnp.sum(matches.astype(jnp.int32) * request_index[None, None, :], axis=2)
    offsets = jnp.arange(LMAX, dtype=jnp.int32)
    live = present[:, :, None] & (offsets[None, None, :] < lengths_row[chosen][:, :, None])
    source_row = jnp.where(
        live, prompt_starts[chosen][:, :, None] + offsets[None, None, :], 0
    ).reshape(peers, slots)
    slot_ids = jnp.where(live, adapter_place_index[chosen][:, :, None], -1).reshape(peers, slots, 1)
    send_rows = jnp.where(
        live.reshape(peers, slots)[:, :, None], tokens[source_row], jnp.zeros((), jnp.bfloat16)
    )
    base_output = jnp.dot(
        lax.all_gather(tokens, "mp", axis=1, tiled=True),
        value_weight,
        preferred_element_type=jnp.float32,
    )
    down_factor_sets = jnp.transpose(adapter_down_weight, (1, 0, 2))

    def mp_total(partial_value):
        return lax.psum(partial_value, "mp")

    adapter_update = grouped_update(
        lax.all_to_all(send_rows, "req", split_axis=0, concat_axis=0, tiled=True),
        lax.all_to_all(slot_ids, "req", split_axis=0, concat_axis=0, tiled=True),
        down_factor_sets,
        adapter_up_weight,
        mp_total,
    )
    value_output = lax.all_to_all(adapter_update, "req", split_axis=0, concat_axis=0, tiled=True)
    position = jnp.arange(tok_rows, dtype=jnp.int32)
    request_of = jnp.sum((position[:, None] >= prompt_ends[None, :]).astype(jnp.int32), axis=1)
    flat_index = (
        owners[request_of] * slots
        + rank_among[request_of] * LMAX
        + position
        - prompt_starts[request_of]
    )
    gathered_terms = value_output.reshape(peers * slots, value_output.shape[2])[flat_index]
    return (base_output + 0.5 * gathered_terms.astype(jnp.float32)).astype(jnp.bfloat16)


def solution(mesh):
    placed = (
        P(("groups", "req"), "mp"),
        P(("groups", "req"), None),
        P(("groups", "req"), None),
        P(("groups", "req")),
        P(None, "mp"),
        P("mp", "req", None),
        P("req", None, "mp"),
    )
    return jax.shard_map(
        body, mesh=mesh, in_specs=placed, out_specs=P(("groups", "req"), "mp"), check_vma=False
    )
```

profile of v0, /device:TPU:0, one launch (start us, length us, event | category | flops | bytes accessed | tf_op | source)
XLA Modules:
  0.0 118.7 jit_solution(14923442569790532206)
XLA Ops:
  6.5 1.0 convert_reduce_fusion.1
  7.5 0.7 iota_compare_fusion.5
  8.2 0.7 fusion.6
  8.9 0.7 and_reduce_fusion
  9.6 0.1 copy.18
  9.6 0.1 reshape.552
  9.7 0.8 copy.21
  10.5 0.2 reduce-window.28
  10.7 0.1 reduce.3
  10.8 0.7 bitcast_subtract_fusion
  11.5 1.5 %gather_fusion.2 = s32[132]{0:T(256)S(1)} fusion(s32[128]{0:T(128)S(1)} %bitcast_subtract_fusion, s32[1024]{0:T(1024)S(1)} %pad_clamp_fusion.6), kind=kCustom, calls=%fused_computation.2 | custom fusion | bytes 1584 | tf_op jit(solution)/shard_map/gather | solution.py:87
  13.0 0.1 reshape.567
  13.1 0.1 add.202
  13.2 0.1 add.203
  13.3 1.6 %gather_fusion = s32[132]{0:T(256)S(1)} fusion(s32[128]{0:T(128)S(1)} %bitcast.49, s32[1024]{0:T(1024)S(1)} %pad_clamp_fusion.6), kind=kCustom, calls=%fused_computation | custom fusion | bytes 1584 | tf_op jit(solution)/shard_map/gather | solution.py:85
  14.9 0.1 reshape.551
  15.0 0.1 lt.150
  15.0 0.1 lt.151
  15.2 0.1 copy.17
  15.3 0.1 and.78
  15.4 0.1 and.79
  15.5 0.1 lt.147
  15.6 1.6 %gather_fusion.1 = s32[132]{0:T(256)S(1)} fusion(s32[128]{0:T(128)S(1)} %copy-done.2, s32[1024]{0:T(1024)S(1)} %pad_clamp_fusion.6), kind=kCustom, calls=%fused_computation.1 | custom fusion | bytes 1584 | tf_op jit(solution)/shard_map/gather | solution.py:89
  17.2 0.1 reshape.559
  17.2 0.1 broadcast_in_dim.60
  17.3 0.1 broadcast_in_dim.61
  17.5 0.6 copy.19
  18.1 6.3 %all-to-all-start = ((s32[4,132,1]{1,2,0:T(1,128)}), s32[4,132,1]{1,2,0:T(1,128)S(1)}, u32[]{:S(2)}, u32[]{:S(2)}) async-start(s32[4,132,1]{1,2,0:T(1,128)} %copy.19), calls=%async_computation | async-start | bytes 8192 | tf_op jit(solution)/shard_map/all_to_all | solution.py:105
  24.4 0.7 all-gather.2.cloned.1.call-update
  25.1 0.1 lt.155
  25.2 0.1 and.83
  25.3 0.2 convert_reduce_fusion
  25.6 3.4 %gather_fusion.3 = bf16[528,1024]{1,0:T(8,128)(2,1)} fusion(bf16[384,1024]{1,0:T(8,128)(2,1)S(1)} %copy-done.4, s32[1024]{0:T(1024)S(1)} %pad_clamp_fusion.5), kind=kCustom, calls=%fused_computation.3 | custom fusion | bytes 2164800 | tf_op jit(solution)/shard_map/gather | solution.py:91
  28.9 2.1 %reshape.575 = bf16[4,132,1024]{2,1,0:T(8,128)(2,1)} reshape(bf16[528,1024]{1,0:T(8,128)(2,1)} %gather_fusion.3) | data formatting | bytes 2162688 | tf_op jit(solution)/shard_map/gather | solution.py:91
  31.1 2.4 %broadcast_select_fusion = bf16[4,132,1024]{2,1,0:T(8,128)(2,1)} fusion(bf16[4,132,1024]{2,1,0:T(8,128)(2,1)} %reshape.575, pred[4,132]{1,0:T(4,128)(4,1)S(1)} %compare_and_fusion), kind=kLoop, calls=%fused_computation.21 | loop fusion | flops 540672 | bytes 2163216 | tf_op jit(solution)/shard_map/jit(_where)/select_n | solution.py:90
  33.6 5.1 %all-to-all-start.1 = ((bf16[4,132,1024]{2,1,0:T(8,128)(2,1)}), bf16[4,132,1024]{2,1,0:T(8,128)(2,1)}, u32[]{:S(2)}, u32[]{:S(2)}) async-start(bf16[4,132,1024]{2,1,0:T(8,128)(2,1)} %broadcast_select_fusion), calls=%async_computation.1 | async-start | bytes 2228224 | tf_op jit(solution)/shard_map/all_to_all | solution.py:104
  38.7 0.1 eq.83
  38.8 0.1 convert_reduce_fusion.2
  38.9 0.2 reduce-window.25
  39.1 1.4 %reduce-window.26 = s32[5,5,128]{2,1,0:T(8,128)S(1)} reduce-window(s32[5,5,128]{2,1,0:T(8,128)S(1)} %reshape.549, s32[]{:T(128)} %constant.19.clone.1), window={size=1x1x128 pad=0_0x0_0x127_0}, to_apply=%region_6.7 | reduce-window | flops 406400 | bytes 25604 | tf_op jit(solution)/shard_map/reduce-window.1
  40.6 0.2 slice_reduce_fusion
  40.8 0.2 reduce-window.27
  41.1 0.1 ge.51
  41.2 0.1 convert_reduce_fusion.3
  41.3 1.8 %gather_fusion.5 = bf16[10,1024,64]{1,2,0:T(8,128)(2,1)} fusion(bf16[5,1024,64]{1,2,0:T(8,128)(2,1)S(1)} %bitcast.54, s32[1024]{0:T(1024)S(1)} %pad_clamp_fusion.4), kind=kCustom, calls=%fused_computation.5 | custom fusion | bytes 2621480 | tf_op jit(solution)/shard_map/gather | solution.py:40
  43.1 0.6 gather_fusion.6
  43.7 0.1 fusion.8
  43.8 4.1 %scatter_custom_fusion.1 = s32[1280]{0:T(1024)S(1)} fusion(s32[528]{0:T(1024)S(1)} %get-tuple-element.6, s32[528]{0:T(1024)S(1)} %iota.53, s32[]{:T(128)} %constant.19.clone.1), kind=kCustom, calls=%fused_computation.59 | custom fusion | bytes 5124 | tf_op jit(solution)/shard_map/scatter | solution.py:28
  47.9 2.5 %scatter_custom_fusion = pred[1280]{0:T(1024)(128)(4,1)S(1)} fusion(s32[528]{0:T(1024)S(1)} %get-tuple-element.6, pred[528]{0:T(1024)(128)(4,1)S(1)} %broadcast.482, pred[]{:T(512)} %constant.20.clone.1), kind=kCustom, calls=%fused_computation.63 | custom fusion | bytes 1281 | tf_op jit(solution)/shard_map/scatter | solution.py:30
  50.5 14.9 %all-to-all-done.1 = bf16[4,132,1024]{2,1,0:T(8,128)(2,1)} async-done(((bf16[4,132,1024]{2,1,0:T(8,128)(2,1)}), bf16[4,132,1024]{2,1,0:T(8,128)(2,1)}, u32[]{:S(2)}, u32[]{:S(2)}) %all-to-all-start.1) | async-done | bytes 1081376 | tf_op jit(solution)/shard_map/all_to_all | solution.py:104
  65.4 1.3 %reshape.546 = bf16[528,1024]{1,0:T(8,128)(2,1)S(1)} reshape(bf16[4,132,1024]{2,1,0:T(8,128)(2,1)} %all-to-all-done.1) | data formatting | bytes 2162688 | tf_op jit(solution)/shard_map/reshape | solution.py:12
  66.7 5.1 %gather_fusion.4 = bf16[1280,1024]{1,0:T(8,128)(2,1)} fusion(bf16[528,1024]{1,0:T(8,128)(2,1)S(1)} %reshape.546, s32[2048]{0:T(1024)S(1)} %pad_clamp_fusion), kind=kCustom, calls=%fused_computation.4 | custom fusion | bytes 5248000 | tf_op jit(solution)/shard_map/gather | solution.py:31
  71.8 3.2 %fusion = f32[10,128,64]{1,2,0:T(8,128)S(1)} fusion(bf16[10,1024,64]{1,2,0:T(8,128)(2,1)} %gather_fusion.5, bf16[10,128,1024]{2,1,0:T(8,128)(2,1)} %bitcast.55, pred[10,128]{1,0:T(8,128)(4,1)S(1)} %bitcast.58), kind=kOutput, calls=%fused_computation.14 | convolution fusion | flops 169082880 | bytes 4261120 | tf_op jit(solution)/shard_map/bkf,bfr->bkr/dot_general | solution.py:37
  75.0 13.6 %all-reduce.2 = bf16[10,128,64]{1,2,0:T(8,128)(2,1)S(1)} all-reduce(f32[10,128,64]{1,2,0:T(8,128)S(1)} %fusion), channel_id=1, replica_groups=mesh['groups'=2,'req'=4,'mp'=4] {'mp'}, use_global_device_ids=true, to_apply=%region_13.14 | all-reduce | flops 81920 | bytes 491520 | tf_op jit(solution)/shard_map/psum | solution.py:101
  88.6 0.4 convolution_convert_fusion
  89.0 2.7 %gather_fusion.7 = bf16[528,256]{1,0:T(8,128)(2,1)S(1)} fusion(bf16[1280,256]{1,0:T(8,128)(2,1)S(1)} %bitcast.53, s32[1024]{0:T(1024)S(1)} %pad_clamp_fusion.3), kind=kCustom, calls=%fused_computation.7 | custom fusion | bytes 542784 | tf_op jit(solution)/shard_map/gather | solution.py:52
  91.8 0.9 broadcast_select_fusion.1
  92.7 3.4 %all-to-all-start.2 = ((bf16[4,132,256]{2,1,0:T(8,128)(2,1)}), bf16[4,132,256]{2,1,0:T(8,128)(2,1)S(1)}, u32[]{:S(2)}, u32[]{:S(2)}) async-start(bf16[4,132,256]{2,1,0:T(8,128)(2,1)} %broadcast_select_fusion.1), calls=%async_computation.2 | async-start | bytes 557056 | tf_op jit(solution)/shard_map/all_to_all | solution.py:110
  96.1 2.7 %gather_fusion.9 = s32[384]{0:T(512)S(1)} fusion(s32[128]{0:T(128)S(1)} %convert_reduce_fusion.1, s32[1024]{0:T(1024)S(1)} %pad_clamp_fusion.2), kind=kCustom, calls=%fused_computation.9 | custom fusion | bytes 4608 | tf_op jit(solution)/shard_map/gather | solution.py:115
  98.8 2.7 %gather_fusion.8 = s32[384]{0:T(512)S(1)} fusion(s32[128]{0:T(128)S(1)} %bitcast.52, s32[1024]{0:T(1024)S(1)} %pad_clamp_fusion.2), kind=kCustom, calls=%fused_computation.8 | custom fusion | bytes 4608 | tf_op jit(solution)/shard_map/gather | solution.py:114
  101.5 2.7 %gather_fusion.10 = s32[384]{0:T(512)S(1)} fusion(s32[128]{0:T(128)S(1)} %bitcast_subtract_fusion, s32[1024]{0:T(1024)S(1)} %pad_clamp_fusion.2), kind=kCustom, calls=%fused_computation.10 | custom fusion | bytes 4608 | tf_op jit(solution)/shard_map/gather | solution.py:117
  104.3 1.9 %all-to-all-done.2 = bf16[4,132,256]{2,1,0:T(8,128)(2,1)S(1)} async-done(((bf16[4,132,256]{2,1,0:T(8,128)(2,1)}), bf16[4,132,256]{2,1,0:T(8,128)(2,1)S(1)}, u32[]{:S(2)}, u32[]{:S(2)}) %all-to-all-start.2) | async-done | bytes 270368 | tf_op jit(solution)/shard_map/all_to_all | solution.py:110
  106.2 2.1 %gather_fusion.11 = bf16[384,256]{1,0:T(8,128)(2,1)S(1)} fusion(bf16[528,256]{1,0:T(8,128)(2,1)S(1)} %reshape.548, s32[1024]{0:T(1024)S(1)} %pad_clamp_fusion.1), kind=kCustom, calls=%fused_computation.11 | custom fusion | bytes 394752 | tf_op jit(solution)/shard_map/gather | solution.py:119
  108.3 3.6 %fusion.4 = bf16[384,256]{1,0:T(8,128)(2,1)} fusion(bf16[384,4096]{1,0:T(8,128)(2,1)} %all-gather.2.cloned.1.call-done, bf16[4096,256]{1,0:T(8,128)(2,1)S(1)} %copy-done, bf16[384,256]{1,0:T(8,128)(2,1)S(1)} %gather_fusion.11), kind=kOutput, calls=%fused_computation.20 | convolution fusion | flops 805699584 | bytes 5636096 | tf_op jit(solution)/shard_map/dot_general | solution.py:93
  (53 shorter events, 0.6 us)
Async XLA Ops:
  6.5 101.8 %copy-start = (bf16[4096,256]{1,0:T(8,128)(2,1)S(1)}, bf16[4096,256]{1,0:T(8,128)(2,1)}, u32[]{:S(2)}) copy-start(bf16[4096,256]{1,0:T(8,128)(2,1)} %param.11) | copy-start | bytes 6291460
  6.5 6.8 %copy-start.1 = (s32[1,128]{1,0:T(1,128)S(1)}, s32[1,128]{1,0:T(1,128)}, u32[]{:S(2)}) copy-start(s32[1,128]{1,0:T(1,128)} %param.8) | copy-start | bytes 1540
  11.4 4.1 %copy-start.2 = (s32[128]{0:T(128)S(1)}, s32[128]{0:T(128)}, u32[]{:S(2)}) copy-start(s32[128]{0:T(128)} %param.10) | copy-start | bytes 1540
  14.9 10.7 %copy-start.4 = (bf16[384,1024]{1,0:T(8,128)(2,1)S(1)}, bf16[384,1024]{1,0:T(8,128)(2,1)}, u32[]{:S(2)}) copy-start(bf16[384,1024]{1,0:T(8,128)(2,1)} %param.7) | copy-start | bytes 2359300
  18.1 15.5 %all-to-all-start = ((s32[4,132,1]{1,2,0:T(1,128)}), s32[4,132,1]{1,2,0:T(1,128)S(1)}, u32[]{:S(2)}, u32[]{:S(2)}) async-start(s32[4,132,1]{1,2,0:T(1,128)} %copy.19), calls=%async_computation | async-start | bytes 8192 | tf_op jit(solution)/shard_map/all_to_all | solution.py:105
  24.4 83.9 %all-gather.2.cloned.1.call-start = ((), (), s32[]{:S(2)}) async-start(), calls=%async_computation.3 | async-start | bytes 3932160 | tf_op jit(solution)/shard_map/all_gather | solution.py:94
  31.1 10.2 %copy-start.5 = (bf16[1024,5,64]{0,2,1:T(8,128)(2,1)S(1)}, bf16[1024,5,64]{0,2,1:T(8,128)(2,1)}, u32[]{:S(2)}) copy-start(bf16[1024,5,64]{0,2,1:T(8,128)(2,1)} %param.12) | copy-start | bytes 1966084
  33.6 31.8 %all-to-all-start.1 = ((bf16[4,132,1024]{2,1,0:T(8,128)(2,1)}), bf16[4,132,1024]{2,1,0:T(8,128)(2,1)}, u32[]{:S(2)}, u32[]{:S(2)}) async-start(bf16[4,132,1024]{2,1,0:T(8,128)(2,1)} %broadcast_select_fusion), calls=%async_computation.1 | async-start | bytes 2228224 | tf_op jit(solution)/shard_map/all_to_all | solution.py:104
  41.3 1.8 %copy-start.6 = (bf16[5,64,256]{2,1,0:T(8,128)(2,1)S(1)}, bf16[5,64,256]{2,1,0:T(8,128)(2,1)}, u32[]{:S(2)}) copy-start(bf16[5,64,256]{2,1,0:T(8,128)(2,1)} %param.13) | copy-start | bytes 491524
  91.7 7.1 %copy-start.3 = (s32[128,1]{0,1:T(1,128)S(1)}, s32[128,1]{0,1:T(1,128)}, u32[]{:S(2)}) copy-start(s32[128,1]{0,1:T(1,128)} %param.9) | copy-start | bytes 1540
  92.7 13.5 %all-to-all-start.2 = ((bf16[4,132,256]{2,1,0:T(8,128)(2,1)}), bf16[4,132,256]{2,1,0:T(8,128)(2,1)S(1)}, u32[]{:S(2)}, u32[]{:S(2)}) async-start(bf16[4,132,256]{2,1,0:T(8,128)(2,1)} %broadcast_select_fusion.1), calls=%async_computation.2 | async-start | bytes 557056 | tf_op jit(solution)/shard_map/all_to_all | solution.py:110
Sparse Core Ops, SparseCore 0:
  26.8 29.9 all-gather.1
where the time goes:
time: 119 us
  local copies, waits for them, and re-layouts  42 us (35%)
  waiting for transfers between devices  17.5 us (15%)
  starting transfers between devices  14.9 us (13%)
  between operations  13.8 us (12%)
  blocking collectives  13.6 us (11%)
  other arithmetic  9.79 us (8%)
  matrix products  7.12 us (6%)
    all_to_all x1, waiting for transfers between devices, body(): lax.all_to_all(send_rows, 'req', split_axis=0, concat_axis=0, tiled=True)  14.9 us
    psum x1, blocking collectives, mp_total(): return lax.psum(partial_value, 'mp')  13.6 us
    all_to_all x1, starting transfers between devices, body(): lax.all_to_all(slot_ids, 'req', split_axis=0, concat_axis=0, tiled=True)  6.32 us
    gather x2, local copies, waits for them, and re-layouts, body(): tokens[source_row]  5.5 us
    all_to_all x1, starting transfers between devices, body(): lax.all_to_all(send_rows, 'req', split_axis=0, concat_axis=0, tiled=True)  5.1 us
    gather x1, local copies, waits for them, and re-layouts, grouped_update(): flat_rows[source]  5.07 us
    scatter x1, local copies, waits for them, and re-layouts, grouped_update(): source = jnp.zeros((grouped,), jnp.int32).at[target].set(jnp.arange(count...  4.1 us
    dot_general x1, matrix products, body(): jnp.dot(lax.all_gather(tokens, 'mp', axis=1, tiled=True), value_weight, p...  3.55 us
  transfers between devices with their start and end apart: 4, of which 2 were waited for; matrix products, arithmetic and copies ran while one was open for 37% of the time, Pallas kernels for 0%

commit v1 on v0

--- a/solution.py
+++ b/solution.py
@@ -1,10 +1,329 @@
+import functools
+
 import jax
 import jax.numpy as jnp
 from jax import lax
+from jax.experimental import pallas as pl
+from jax.experimental.pallas import tpu as pltpu
 from jax.sharding import PartitionSpec as P
 
 LMAX = 4
 REQ_DEV = 128
+GATHER_BYTES = 24 << 20
+
+PIECES = 4
+SLICES = 4
+MESH = pl.DeviceIdType.MESH
+
+
+def adapter_kernel(
+    peers,
+    held,
+    rank,
+    tok,
+    lengths,
+    holder,
+    place,
+    weight,
+    down,
+    up,
+    out,
+    tok_all,
+    weight_here,
+    down_all,
+    up_all,
+    low_all,
+    base,
+    low_sum,
+    adapter_of,
+    local_sem,
+    z_send_sem,
+    z_recv_sem,
+    y_send_sem,
+    y_recv_sem,
+    x_send_sem,
+    x_recv_sem,
+    low_send_sem,
+    low_recv_sem,
+):
+    rows, feats = tok.shape
+    cols = out.shape[1]
+    width = held * rank
+    half = rows // 2
+    piece = feats // (2 * PIECES)
+    batch = rows // SLICES
+    g, z, m = lax.axis_index("groups"), lax.axis_index("req"), lax.axis_index("mp")
+    sibling = m + 1 - 2 * lax.rem(m, 2)
+    across = lax.rem(m + 2, 4)
+    diagonal = lax.rem(sibling + 2, 4)
+
+    def remote(src, dst, send_sem, recv_sem, device):
+        return pltpu.make_async_remote_copy(
+            src_ref=src,
+            dst_ref=dst,
+            send_sem=send_sem,
+            recv_sem=recv_sem,
+            device_id=device,
+            device_id_type=MESH,
+        )
+
+    def strip(h, side, c):
+        if c < PIECES:
+            lanes = pl.ds(pl.multiple_of(side * (feats // 2) + c * piece, 128), piece)
+            return down_all.at[h, :, lanes]
+        lanes = pl.ds(pl.multiple_of(side * (cols // 2), 128), cols // 2)
+        return up_all.at[h, :, lanes]
+
+    def own_strip(c):
+        if c < PIECES:
+            lanes = pl.ds(pl.multiple_of(g * (feats // 2) + c * piece, 128), piece)
+            return down.at[:, lanes]
+        lanes = pl.ds(pl.multiple_of(g * (cols // 2), 128), cols // 2)
+        return up.at[:, lanes]
+
+    def step_of(way):
+        return 1 if way == 0 else -1
+
+    def has(way, d):
+        return z >= d if way == 0 else z + d <= peers - 1
+
+    def has_next(way):
+        return z + 1 <= peers - 1 if way == 0 else z >= 1
+
+    def z_send(way, d, c):
+        h = z - step_of(way) * d
+        target = strip(h, g, c)
+        return remote(
+            own_strip(c) if d == 0 else target,
+            target,
+            z_send_sem.at[way, d, c],
+            z_recv_sem.at[way, d, c],
+            {"req": z + step_of(way)},
+        )
+
+    def z_recv(way, d, c):
+        target = strip(z - step_of(way) * d, g, c)
+        return remote(
+            target,
+            target,
+            z_send_sem.at[way, d - 1, c],
+            z_recv_sem.at[way, d - 1, c],
+            {"req": z - step_of(way)},
+        )
+
+    def y_copy(way, d, c, side):
+        target = strip(z - step_of(way) * d, side, c)
+        return remote(
+            target,
+            target,
+            y_send_sem.at[way, d - 1, c],
+            y_recv_sem.at[way, d - 1, c],
+            {"groups": 1 - g},
+        )
+
+    def pass_on(way, d, c):
+        @pl.when(has(way, d))
+        def _():
+            z_recv(way, d, c).wait_recv()
+            if d < peers - 1:
+                pl.when(has_next(way))(z_send(way, d, c).start)
+            y_copy(way, d, c, g).start()
+
+    def batch_of(b, s):
+        return tok_all.at[b, pl.ds(s * batch, batch)]
+
+    def x_copy(kind, s):
+        if kind == 2:
+            src = batch_of(across, s)
+        else:
+            src = tok.at[pl.ds(s * batch, batch)]
+        return remote(
+            src,
+            batch_of(across if kind == 2 else m, s),
+            x_send_sem.at[kind, s],
+            x_recv_sem.at[kind, s],
+            {"mp": across if kind == 0 else sibling},
+        )
+
+    def x_recv(kind, s):
+        target = batch_of((across, sibling, diagonal)[kind], s)
+        return remote(
+            target,
+            target,
+            x_send_sem.at[kind, s],
+            x_recv_sem.at[kind, s],
+            {"mp": across if kind == 0 else sibling},
+        )
+
+    def low_copy(i, b):
+        return remote(
+            low_all.at[m],
+            low_all.at[m if b is None else b],
+            low_send_sem.at[i],
+            low_recv_sem.at[i],
+            {"mp": (across, sibling, diagonal)[i]},
+        )
+
+    local = [
+        pltpu.make_async_copy(tok, tok_all.at[m], local_sem.at[0]),
+        pltpu.make_async_copy(down, down_all.at[z], local_sem.at[1]),
+        pltpu.make_async_copy(weight, weight_here, local_sem.at[2]),
+        pltpu.make_async_copy(up, up_all.at[z], local_sem.at[3]),
+    ]
+    for copy in local:
+        copy.start()
+
+    barrier = pltpu.get_barrier_semaphore()
+    for device in ({"mp": across}, {"mp": sibling}, {"mp": diagonal}, {"groups": 1 - g}):
+        pl.semaphore_signal(barrier, inc=1, device_id=device, device_id_type=MESH)
+    for way in range(2):
+
+        @pl.when(has_next(way))
+        def _(way=way):
+            pl.semaphore_signal(
+                barrier, inc=1, device_id={"req": z + step_of(way)}, device_id_type=MESH
+            )
+
+    prompts = lengths.shape[1]
+    lens = lengths[...]
+    earlier = lax.broadcasted_iota(jnp.int32, (prompts, prompts), 0) <= lax.broadcasted_iota(
+        jnp.int32, (prompts, prompts), 1
+    )
+    ends = jnp.dot(
+        jnp.broadcast_to(lens, (8, prompts)).astype(jnp.float32).astype(jnp.bfloat16),
+        earlier.astype(jnp.float32).astype(jnp.bfloat16),
+        preferred_element_type=jnp.float32,
+    )[0:1].astype(jnp.int32)
+    position = lax.broadcasted_iota(jnp.int32, (rows, prompts), 0)
+    inside = (position < ends) & (position >= ends - lens)
+    named = jnp.where(inside, holder[...] * held + place[...], 0)
+    adapter_of[...] = jnp.sum(named, axis=1, keepdims=True)
+
+    beside = lax.div(z + peers - 1, peers) + lax.div(2 * peers - 2 - z, peers)
+    pl.semaphore_wait(barrier, 4 + beside)
+
+    for c in range(PIECES):
+        for way in range(2):
+            pl.when(has_next(way))(z_send(way, 0, c).start)
+    for s in range(SLICES):
+        x_copy(0, s).start()
+    for s in range(SLICES):
+        x_copy(1, s).start()
+
+    def add_base(b, first=False):
+        term = jnp.dot(
+            tok_all[b],
+            weight_here[pl.ds(pl.multiple_of(b * feats, 128), feats)],
+            preferred_element_type=jnp.float32,
+        )
+        if first:
+            base[...] = term
+        else:
+            base[...] += term
+
+    lane = lax.broadcasted_iota(jnp.int32, (1, width), 1)
+
+    def member(h, part):
+        return adapter_of[part * half : (part + 1) * half, :] == lane // rank + h * held
+
+    def fold(part, turned):
+        shape = (2 * rank, width) if turned else (width, 2 * rank)
+        one = lax.broadcasted_iota(jnp.int32, shape, 1 if turned else 0)
+        two = lax.broadcasted_iota(jnp.int32, shape, 0 if turned else 1)
+        return (lax.rem(one, rank) == two - part * rank).astype(jnp.float32).astype(jnp.bfloat16)
+
+    def add_low(h, first=False):
+        total = jnp.zeros((half, 2 * rank), jnp.float32)
+        for part in range(2):
+            partial = lax.dot_general(
+                tok_all[m, part * half : (part + 1) * half],
+                down_all[h],
+                (((1,), (1,)), ((), ())),
+                preferred_element_type=jnp.float32,
+            )
+            kept = jnp.where(member(h, part), partial, 0.0).astype(jnp.bfloat16)
+            total += jnp.dot(kept, fold(part, False), preferred_element_type=jnp.float32)
+        if first:
+            low_sum[...] = total
+        else:
+            low_sum[...] += total
+
+    def finish(way, d):
+        @pl.when(has(way, d))
+        def _():
+            for c in range(PIECES):
+                y_copy(way, d, c, 1 - g).wait_recv()
+            add_low(z - step_of(way) * d)
+
+    local[0].wait()
+    local[1].wait()
+    add_low(z, first=True)
+    local[2].wait()
+    add_base(m, first=True)
+    slot = 0
+    for d in range(1, peers):
+        for c in range(PIECES):
+            for way in range(2):
+                pass_on(way, d, c)
+            if slot < SLICES:
+                x_recv(0, slot).wait_recv()
+                x_copy(2, slot).start()
+            slot += 1
+        if d == 1:
+            for s in range(SLICES):
+                x_recv(1, s).wait_recv()
+            add_base(sibling)
+            add_base(across)
+        if d == 2:
+            for s in range(SLICES):
+                x_recv(2, s).wait_recv()
+            add_base(diagonal)
+        if d >= 2:
+            for way in range(2):
+                finish(way, d - 1)
+    for way in range(2):
+        pl.when(has_next(way))(z_send(way, 0, PIECES).start)
+    for way in range(2):
+        finish(way, peers - 1)
+
+    low_all[m] = low_sum[...].astype(jnp.bfloat16)
+    for i in range(3):
+        low_copy(i, None).start()
+    for d in range(1, peers):
+        for way in range(2):
+            pass_on(way, d, PIECES)
+    for i, b in enumerate((across, sibling, diagonal)):
+        low_copy(i, b).wait_recv()
+    local[3].wait()
+    low = low_all[0].astype(jnp.float32)
+    for b in range(1, 4):
+        low += low_all[b].astype(jnp.float32)
+    low = low.astype(jnp.bfloat16)
+    for d in range(1, peers):
+        for way in range(2):
+            pl.when(has(way, d))(y_copy(way, d, PIECES, 1 - g).wait_recv)
+    for part in range(2):
+        spread = jnp.dot(low, fold(part, True), preferred_element_type=jnp.float32)
+        term = jnp.zeros((half, cols), jnp.float32)
+        for h in range(peers):
+            kept = jnp.where(member(h, part), spread, 0.0).astype(jnp.bfloat16)
+            term += jnp.dot(kept, up_all[h], preferred_element_type=jnp.float32)
+        term = term.astype(jnp.bfloat16).astype(jnp.float32)
+        here = pl.ds(part * half, half)
+        out[here, :] = (base[here, :] + 0.5 * term).astype(jnp.bfloat16)
+
+    for s in range(SLICES):
+        for kind in range(3):
+            x_copy(kind, s).wait_send()
+    for i in range(3):
+        low_copy(i, None).wait_send()
+    for way in range(2):
+        for c in range(PIECES + 1):
+            for d in range(peers - 1):
+                sent = has_next(way) if d == 0 else has_next(way) & has(way, d)
+                pl.when(sent)(z_send(way, d, c).wait_send)
+            for d in range(1, peers):
+                pl.when(has(way, d))(y_copy(way, d, c, g).wait_send)
 
 
 def grouped_update(token_rows, slot_ids, down_factor_sets, up_sets, reduce_fn):
@@ -120,6 +439,60 @@
     return (base_output + 0.5 * gathered_terms.astype(jnp.float32)).astype(jnp.bfloat16)
 
 
+def gather_body(mesh, *args):
+    tokens, lengths, holder, place, value_weight, down, up = args
+    peers, mp = mesh.shape["req"], mesh.shape["mp"]
+    rows, feats = tokens.shape
+    held, rank, cols = up.shape
+    down_rows = jnp.transpose(down, (1, 2, 0)).reshape(held * rank, feats)
+    up_rows = up.reshape(held * rank, cols)
+    anywhere = pl.BlockSpec(memory_space=pl.ANY)
+    vmem = pl.BlockSpec(memory_space=pltpu.VMEM)
+    dma = pltpu.SemaphoreType.DMA
+    hops = max(peers - 1, 1)
+    return pl.pallas_call(
+        functools.partial(adapter_kernel, peers, held, rank),
+        out_shape=jax.ShapeDtypeStruct((rows, cols), jnp.bfloat16),
+        in_specs=[anywhere, vmem, vmem, vmem, anywhere, anywhere, anywhere],
+        out_specs=vmem,
+        scratch_shapes=[
+            pltpu.VMEM((mp, rows, feats), jnp.bfloat16),
+            pltpu.VMEM(value_weight.shape, jnp.bfloat16),
+            pltpu.VMEM((peers, held * rank, feats), jnp.bfloat16),
+            pltpu.VMEM((peers, held * rank, cols), jnp.bfloat16),
+            pltpu.VMEM((mp, rows // 2, 2 * rank), jnp.bfloat16),
+            pltpu.VMEM((rows, cols), jnp.float32),
+            pltpu.VMEM((rows // 2, 2 * rank), jnp.float32),
+            pltpu.VMEM((rows, 1), jnp.int32),
+            dma((4,)),
+            dma((2, hops, PIECES + 1)),
+            dma((2, hops, PIECES + 1)),
+            dma((2, hops, PIECES + 1)),
+            dma((2, hops, PIECES + 1)),
+            dma((3, SLICES)),
+            dma((3, SLICES)),
+            dma((3,)),
+            dma((3,)),
+        ],
+        compiler_params=pltpu.CompilerParams(
+            collective_id=0, has_side_effects=True, vmem_limit_bytes=48 << 20
+        ),
+        cost_estimate=pl.CostEstimate(
+            flops=2 * rows * feats * (mp * cols + peers * held * rank),
+            bytes_accessed=2 * (rows * feats + value_weight.size + down.size + up.size),
+            transcendentals=0,
+        ),
+    )(
+        tokens,
+        lengths,
+        holder.reshape(1, -1),
+        place.reshape(1, -1),
+        value_weight,
+        down_rows,
+        up_rows,
+    )
+
+
 def solution(mesh):
     placed = (
         P(("groups", "req"), "mp"),
@@ -130,6 +503,17 @@
         P("mp", "req", None),
         P("req", None, "mp"),
     )
-    return jax.shard_map(
-        body, mesh=mesh, in_specs=placed, out_specs=P(("groups", "req"), "mp"), check_vma=False
-    )
+
+    def whole(*args):
+        peers = mesh.shape["req"]
+        moved = 2 * (args[5].size // mesh.shape["mp"] + args[6].size // mesh.shape["mp"])
+        fits = moved <= GATHER_BYTES and peers > 1
+        if fits and mesh.shape["mp"] == 4 and mesh.shape["groups"] == 2:
+            part = functools.partial(gather_body, mesh)
+        else:
+            part = body
+        return jax.shard_map(
+            part, mesh=mesh, in_specs=placed, out_specs=P(("groups", "req"), "mp"), check_vma=False
+        )(*args)
+
+    return whole

time: 119 us -> 59.2 us (0.50)
  Pallas kernels: 0 us -> 51.5 us
  local copies, waits for them, and re-layouts: 42 us -> 7.37 us
  waiting for transfers between devices: 17.5 us -> 0 us
  starting transfers between devices: 14.9 us -> 0 us
  between operations: 13.8 us -> 0.02 us
  blocking collectives: 13.6 us -> 0 us
  other arithmetic: 9.79 us -> 0 us
  matrix products: 7.12 us -> 0 us
    pallas_call x0 -> x1, Pallas kernels: none -> 51.5 us  [gather_body(): pl.pallas_call(functools.partial(adapter_kernel, peers, held, rank), out_...]
    gather x17 -> x0, local copies, waits for them, and re-layouts: 30.7 us -> none  [the longest x2 5.5 us: body(): tokens[source_row]]
    all_to_all x3 -> x0, waiting for transfers between devices: 16.8 us -> none  [the longest x1 14.9 us: body(): lax.all_to_all(send_rows, 'req', split_axis=0, concat_axis=0, tiled=True)]
    all_to_all x3 -> x0, starting transfers between devices: 14.9 us -> none  [the longest x1 6.32 us: body(): lax.all_to_all(slot_ids, 'req', split_axis=0, concat_axis=0, tiled=True)]
    psum x1 -> x0, blocking collectives: 13.6 us -> none  [mp_total(): return lax.psum(partial_value, 'mp')]
    unnamed x15, local copies, waits for them, and re-layouts: 0.04 us -> 7.37 us
    dot_general x3 -> x0, matrix products: 7.12 us -> none  [the longest x1 3.55 us: body(): jnp.dot(lax.all_gather(tokens, 'mp', axis=1, tiled=True), value_weight, p...]
    scatter x2 -> x0, local copies, waits for them, and re-layouts: 6.62 us -> none  [the longest x1 4.1 us: grouped_update(): source = jnp.zeros((grouped,), jnp.int32).at[target].set(jnp.arange(count...]
  transfers between devices with their start and end apart: 4 -> 0, of which waited for: 2 -> 0; matrix products, arithmetic and copies ran while one was open for 37% -> 0% of each run, Pallas kernels for 0% -> 0%
where the time goes in v1:
time: 59.2 us; the launch traced here: 58.9 us
  Pallas kernels  51.5 us (87%)
  local copies, waits for them, and re-layouts  7.37 us (12%)
    pallas_call x1, Pallas kernels, gather_body(): pl.pallas_call(functools.partial(adapter_kernel, peers, held, rank), out_...  51.5 us
    unnamed x15, local copies, waits for them, and re-layouts  7.37 us

profile of v1, /device:TPU:0, one launch (start us, length us, event | category | flops | bytes accessed | tf_op | source)
XLA Modules:
  0.0 58.9 jit_solution(17870935136591303984)
XLA Ops:
  0.0 0.0 copy-start
  0.0 1.6 %copy-done = bf16[4096,256]{1,0:T(8,128)(2,1)S(1)} copy-done((bf16[4096,256]{1,0:T(8,128)(2,1)S(1)}, bf16[4096,256]{1,0:T(8,128)(2,1)}, u32[]{:S(2)}) %copy-start) | copy-done | bytes 2097176
  1.6 0.0 copy-start.1
  1.6 1.1 %copy-done.1 = bf16[384,1024]{1,0:T(8,128)(2,1)S(1)} copy-done((bf16[384,1024]{1,0:T(8,128)(2,1)S(1)}, bf16[384,1024]{1,0:T(8,128)(2,1)}, u32[]{:S(2)}) %copy-start.1) | copy-done | bytes 786456
  2.7 0.0 copy-start.2
  2.7 1.1 %copy-done.2 = bf16[1024,5,64]{0,2,1:T(8,128)(2,1)S(1)} copy-done((bf16[1024,5,64]{0,2,1:T(8,128)(2,1)S(1)}, bf16[1024,5,64]{0,2,1:T(8,128)(2,1)}, u32[]{:S(2)}) %copy-start.2) | copy-done | bytes 655384
  3.8 0.0 copy-start.3
  3.8 0.9 %copy-done.3 = bf16[5,64,256]{2,1,0:T(8,128)(2,1)S(1)} copy-done((bf16[5,64,256]{2,1,0:T(8,128)(2,1)S(1)}, bf16[5,64,256]{2,1,0:T(8,128)(2,1)}, u32[]{:S(2)}) %copy-start.3) | copy-done | bytes 163864
  4.7 0.0 copy-start.4
  4.7 0.7 %copy-done.4 = s32[1,128]{1,0:T(1,128)S(1)} copy-done((s32[1,128]{1,0:T(1,128)S(1)}, s32[1,128]{1,0:T(1,128)}, u32[]{:S(2)}) %copy-start.4) | copy-done | bytes 536
  5.4 0.0 copy-start.5
  5.4 0.7 %copy-done.5 = s32[128,1]{0,1:T(1,128)S(1)} copy-done((s32[128,1]{0,1:T(1,128)S(1)}, s32[128,1]{0,1:T(1,128)}, u32[]{:S(2)}) %copy-start.5) | copy-done | bytes 536
  6.0 0.0 copy-start.6
  6.0 0.7 %copy-done.6 = s32[128]{0:T(128)S(1)} copy-done((s32[128]{0:T(128)S(1)}, s32[128]{0:T(128)}, u32[]{:S(2)}) %copy-start.6) | copy-done | bytes 536
  6.7 51.5 %shard_map.73 = bf16[384,256]{1,0:T(8,128)(2,1)S(1)} custom-call(bf16[384,1024]{1,0:T(8,128)(2,1)S(1)} %copy-done.1, s32[1,128]{1,0:T(1,128)S(1)} %copy-done.4, s32[1,128]{1,0:T(1,128)S(1)} %bitcast.8, s32[1,128]{1,0:T(1,128)S(1)} %bitcast.9, bf16[4096,256]{1,0:T(8,128)(2,1)S(1)} %copy-done, bf16[320,1024]{1,0:T(8,128)(2,1)S(1)} %bitcast.6, ...), custom_call_target="tpu_custom_call" | custom-call | flops 1811939328 | bytes 3702784 | tf_op jit(solution)/shard_map/pallas_call | solution.py:453
  58.2 0.7 %copy.9 = bf16[384,256]{1,0:T(8,128)(2,1)} copy(bf16[384,256]{1,0:T(8,128)(2,1)S(1)} %shard_map.73) | data formatting | bytes 393216
Async XLA Ops:
  0.0 1.6 %copy-start = (bf16[4096,256]{1,0:T(8,128)(2,1)S(1)}, bf16[4096,256]{1,0:T(8,128)(2,1)}, u32[]{:S(2)}) copy-start(bf16[4096,256]{1,0:T(8,128)(2,1)} %weight.1) | copy-start | bytes 6291460
  1.6 1.1 %copy-start.1 = (bf16[384,1024]{1,0:T(8,128)(2,1)S(1)}, bf16[384,1024]{1,0:T(8,128)(2,1)}, u32[]{:S(2)}) copy-start(bf16[384,1024]{1,0:T(8,128)(2,1)} %tok.1) | copy-start | bytes 2359300
  2.7 1.1 %copy-start.2 = (bf16[1024,5,64]{0,2,1:T(8,128)(2,1)S(1)}, bf16[1024,5,64]{0,2,1:T(8,128)(2,1)}, u32[]{:S(2)}) copy-start(bf16[1024,5,64]{0,2,1:T(8,128)(2,1)} %param.12) | copy-start | bytes 1966084
  3.8 0.9 %copy-start.3 = (bf16[5,64,256]{2,1,0:T(8,128)(2,1)S(1)}, bf16[5,64,256]{2,1,0:T(8,128)(2,1)}, u32[]{:S(2)}) copy-start(bf16[5,64,256]{2,1,0:T(8,128)(2,1)} %param.13) | copy-start | bytes 491524
  4.7 0.7 %copy-start.4 = (s32[1,128]{1,0:T(1,128)S(1)}, s32[1,128]{1,0:T(1,128)}, u32[]{:S(2)}) copy-start(s32[1,128]{1,0:T(1,128)} %lengths.1) | copy-start | bytes 1540
  5.4 0.7 %copy-start.5 = (s32[128,1]{0,1:T(1,128)S(1)}, s32[128,1]{0,1:T(1,128)}, u32[]{:S(2)}) copy-start(s32[128,1]{0,1:T(1,128)} %param.9) | copy-start | bytes 1540
  6.0 0.7 %copy-start.6 = (s32[128]{0:T(128)S(1)}, s32[128]{0:T(128)}, u32[]{:S(2)}) copy-start(s32[128]{0:T(128)} %param.10) | copy-start | bytes 1540

commit v2 on v1

--- a/solution.py
+++ b/solution.py
@@ -29,14 +29,22 @@
     up,
     out,
     tok_all,
+    tok_other,
     weight_here,
     down_all,
     up_all,
     low_all,
+    low_sent,
     base,
     low_sum,
+    small,
+    prompts_of,
     adapter_of,
     local_sem,
+    prompt_send_sem,
+    prompt_recv_sem,
+    t_send_sem,
+    t_recv_sem,
     z_send_sem,
     z_recv_sem,
     y_send_sem,
@@ -48,9 +56,11 @@
 ):
     rows, feats = tok.shape
     cols = out.shape[1]
-    width = held * rank
-    half = rows // 2
-    piece = feats // (2 * PIECES)
+    part_rank = rank // 2
+    packed = 2 * rank // part_rank
+    width = held * part_rank
+    quarter = rows // packed
+    piece = feats // PIECES
     batch = rows // SLICES
     g, z, m = lax.axis_index("groups"), lax.axis_index("req"), lax.axis_index("mp")
     sibling = m + 1 - 2 * lax.rem(m, 2)
@@ -69,15 +79,16 @@
 
     def strip(h, side, c):
         if c < PIECES:
-            lanes = pl.ds(pl.multiple_of(side * (feats // 2) + c * piece, 128), piece)
-            return down_all.at[h, :, lanes]
+            return down_all.at[h, :, :, pl.ds(c * piece, piece)]
         lanes = pl.ds(pl.multiple_of(side * (cols // 2), 128), cols // 2)
         return up_all.at[h, :, lanes]
 
+    def ranks_of(side):
+        return pl.ds(pl.multiple_of(side * part_rank, 16), part_rank)
+
     def own_strip(c):
         if c < PIECES:
-            lanes = pl.ds(pl.multiple_of(g * (feats // 2) + c * piece, 128), piece)
-            return down.at[:, lanes]
+            return down.at[:, ranks_of(g), pl.ds(c * piece, piece)]
         lanes = pl.ds(pl.multiple_of(g * (cols // 2), 128), cols // 2)
         return up.at[:, lanes]
 
@@ -86,6 +97,9 @@
 
     def has(way, d):
         return z >= d if way == 0 else z + d <= peers - 1
+
+    def upstream(way):
+        return z if way == 0 else peers - 1 - z
 
     def has_next(way):
         return z + 1 <= peers - 1 if way == 0 else z >= 1
@@ -111,23 +125,34 @@
             {"req": z - step_of(way)},
         )
 
-    def y_copy(way, d, c, side):
-        target = strip(z - step_of(way) * d, side, c)
+    def y_copy(way, d, side):
+        target = strip(z - step_of(way) * d, side, PIECES)
         return remote(
             target,
             target,
-            y_send_sem.at[way, d - 1, c],
-            y_recv_sem.at[way, d - 1, c],
+            y_send_sem.at[way, d - 1],
+            y_recv_sem.at[way, d - 1],
             {"groups": 1 - g},
         )
 
-    def pass_on(way, d, c):
-        @pl.when(has(way, d))
+    def t_copy(s):
+        there = pl.ds(s * batch, batch)
+        return remote(
+            tok.at[there],
+            tok_other.at[there],
+            t_send_sem.at[s],
+            t_recv_sem.at[s],
+            {"groups": 1 - g},
+        )
+
+    def pass_on(way, d, c, when):
+        @pl.when(when)
         def _():
             z_recv(way, d, c).wait_recv()
             if d < peers - 1:
                 pl.when(has_next(way))(z_send(way, d, c).start)
-            y_copy(way, d, c, g).start()
+            if c == PIECES:
+                y_copy(way, d, g).start()
 
     def batch_of(b, s):
         return tok_all.at[b, pl.ds(s * batch, batch)]
@@ -155,26 +180,36 @@
             {"mp": across if kind == 0 else sibling},
         )
 
-    def low_copy(i, b):
+    others = (across, sibling, diagonal)
+    low_device = [{"mp": b} for b in others] + [{"groups": 1 - g, "mp": b} for b in others + (m,)]
+
+    def low_copy(i):
         return remote(
-            low_all.at[m],
-            low_all.at[m if b is None else b],
+            low_sent.at[0 if i < 3 else 1],
+            low_all.at[g, m],
             low_send_sem.at[i],
             low_recv_sem.at[i],
-            {"mp": (across, sibling, diagonal)[i]},
-        )
+            low_device[i],
+        )
+
+    def low_recv(i):
+        target = low_all.at[g if i < 3 else 1 - g, (others + others + (m,))[i]]
+        return remote(target, target, low_send_sem.at[i], low_recv_sem.at[i], low_device[i])
 
     local = [
-        pltpu.make_async_copy(tok, tok_all.at[m], local_sem.at[0]),
-        pltpu.make_async_copy(down, down_all.at[z], local_sem.at[1]),
-        pltpu.make_async_copy(weight, weight_here, local_sem.at[2]),
-        pltpu.make_async_copy(up, up_all.at[z], local_sem.at[3]),
+        pltpu.make_async_copy(lengths, small.at[0], local_sem.at[0]),
+        pltpu.make_async_copy(holder, small.at[1], local_sem.at[1]),
+        pltpu.make_async_copy(place, small.at[2], local_sem.at[2]),
+        pltpu.make_async_copy(tok, tok_all.at[m], local_sem.at[3]),
+        pltpu.make_async_copy(down.at[:, ranks_of(g)], down_all.at[z], local_sem.at[4]),
+        pltpu.make_async_copy(weight, weight_here, local_sem.at[5]),
+        pltpu.make_async_copy(up, up_all.at[z], local_sem.at[6]),
     ]
     for copy in local:
         copy.start()
 
     barrier = pltpu.get_barrier_semaphore()
-    for device in ({"mp": across}, {"mp": sibling}, {"mp": diagonal}, {"groups": 1 - g}):
+    for device in low_device:
         pl.semaphore_signal(barrier, inc=1, device_id=device, device_id_type=MESH)
     for way in range(2):
 
@@ -185,30 +220,52 @@
             )
 
     prompts = lengths.shape[1]
-    lens = lengths[...]
-    earlier = lax.broadcasted_iota(jnp.int32, (prompts, prompts), 0) <= lax.broadcasted_iota(
-        jnp.int32, (prompts, prompts), 1
-    )
-    ends = jnp.dot(
-        jnp.broadcast_to(lens, (8, prompts)).astype(jnp.float32).astype(jnp.bfloat16),
-        earlier.astype(jnp.float32).astype(jnp.bfloat16),
-        preferred_element_type=jnp.float32,
-    )[0:1].astype(jnp.int32)
-    position = lax.broadcasted_iota(jnp.int32, (rows, prompts), 0)
-    inside = (position < ends) & (position >= ends - lens)
-    named = jnp.where(inside, holder[...] * held + place[...], 0)
-    adapter_of[...] = jnp.sum(named, axis=1, keepdims=True)
+    for copy in local[:3]:
+        copy.wait()
+    lens = small[0]
+    adapter = small[1] * held + small[2]
+    row = lax.broadcasted_iota(jnp.int32, (8, prompts), 0)
+    prompts_of[0] = jnp.where(row == 0, lens, adapter)
 
     beside = lax.div(z + peers - 1, peers) + lax.div(2 * peers - 2 - z, peers)
-    pl.semaphore_wait(barrier, 4 + beside)
+    pl.semaphore_wait(barrier, 7 + beside)
 
     for c in range(PIECES):
         for way in range(2):
             pl.when(has_next(way))(z_send(way, 0, c).start)
+    for way in range(2):
+        pl.when(has_next(way) & (upstream(way) == 0))(z_send(way, 0, PIECES).start)
+    prompt_copy = remote(
+        prompts_of.at[0],
+        prompts_of.at[1],
+        prompt_send_sem.at[0],
+        prompt_recv_sem.at[0],
+        {"groups": 1 - g},
+    )
+    prompt_copy.start()
     for s in range(SLICES):
         x_copy(0, s).start()
     for s in range(SLICES):
+        t_copy(s).start()
+    for s in range(SLICES):
         x_copy(1, s).start()
+
+    def name_adapters(which):
+        lens = prompts_of[which, 0:1]
+        earlier = lax.broadcasted_iota(jnp.int32, (prompts, prompts), 0) <= lax.broadcasted_iota(
+            jnp.int32, (prompts, prompts), 1
+        )
+        ends = jnp.dot(
+            jnp.broadcast_to(lens, (8, prompts)).astype(jnp.float32).astype(jnp.bfloat16),
+            earlier.astype(jnp.float32).astype(jnp.bfloat16),
+            preferred_element_type=jnp.float32,
+        )[0:1].astype(jnp.int32)
+        position = lax.broadcasted_iota(jnp.int32, (rows, prompts), 0)
+        inside = (position < ends) & (position >= ends - lens)
+        named = jnp.where(inside, prompts_of[which, 1:2], 0)
+        adapter_of[which] = jnp.sum(named, axis=1, keepdims=True)
+
+    name_adapters(0)
 
     def add_base(b, first=False):
         term = jnp.dot(
@@ -221,109 +278,132 @@
         else:
             base[...] += term
 
-    lane = lax.broadcasted_iota(jnp.int32, (1, width), 1)
-
-    def member(h, part):
-        return adapter_of[part * half : (part + 1) * half, :] == lane // rank + h * held
-
-    def fold(part, turned):
-        shape = (2 * rank, width) if turned else (width, 2 * rank)
-        one = lax.broadcasted_iota(jnp.int32, shape, 1 if turned else 0)
-        two = lax.broadcasted_iota(jnp.int32, shape, 0 if turned else 1)
-        return (lax.rem(one, rank) == two - part * rank).astype(jnp.float32).astype(jnp.bfloat16)
-
-    def add_low(h, first=False):
-        total = jnp.zeros((half, 2 * rank), jnp.float32)
-        for part in range(2):
-            partial = lax.dot_general(
-                tok_all[m, part * half : (part + 1) * half],
-                down_all[h],
-                (((1,), (1,)), ((), ())),
-                preferred_element_type=jnp.float32,
+    def member(which, h, part, per):
+        lane = lax.broadcasted_iota(jnp.int32, (1, held * per), 1)
+        owned = adapter_of[which, part * quarter : (part + 1) * quarter, :]
+        return owned == lane // per + h * held
+
+    def ones(shape, test):
+        one, two = (lax.broadcasted_iota(jnp.int32, shape, axis) for axis in range(2))
+        return test(one, two).astype(jnp.float32).astype(jnp.bfloat16)
+
+    def add_low(which, h, first=False):
+        partial = lax.dot_general(
+            tok_all[m] if which == 0 else tok_other[...],
+            down_all[h].reshape(width, feats),
+            (((1,), (1,)), ((), ())),
+            preferred_element_type=jnp.float32,
+        )
+        total = jnp.zeros((quarter, 2 * rank), jnp.float32)
+        for part in range(packed):
+            mine = partial[part * quarter : (part + 1) * quarter]
+            kept = jnp.where(member(which, h, part, part_rank), mine, 0.0).astype(jnp.bfloat16)
+            place_in = ones(
+                (width, 2 * rank),
+                lambda j, i: lax.rem(j, part_rank) == i - part * part_rank,
             )
-            kept = jnp.where(member(h, part), partial, 0.0).astype(jnp.bfloat16)
-            total += jnp.dot(kept, fold(part, False), preferred_element_type=jnp.float32)
+            total += jnp.dot(kept, place_in, preferred_element_type=jnp.float32)
         if first:
-            low_sum[...] = total
+            low_sum[which] = total
         else:
-            low_sum[...] += total
-
-    def finish(way, d):
+            low_sum[which] += total
+
+    def add_held(which, way, d):
         @pl.when(has(way, d))
         def _():
-            for c in range(PIECES):
-                y_copy(way, d, c, 1 - g).wait_recv()
-            add_low(z - step_of(way) * d)
-
-    local[0].wait()
-    local[1].wait()
-    add_low(z, first=True)
-    local[2].wait()
+            add_low(which, z - step_of(way) * d)
+
+    local[3].wait()
+    local[4].wait()
+    add_low(0, z, first=True)
+    local[5].wait()
     add_base(m, first=True)
     slot = 0
     for d in range(1, peers):
         for c in range(PIECES):
             for way in range(2):
-                pass_on(way, d, c)
+                pass_on(way, d, c, has(way, d))
             if slot < SLICES:
                 x_recv(0, slot).wait_recv()
                 x_copy(2, slot).start()
             slot += 1
+        for way in range(2):
+            pl.when(has_next(way) & (upstream(way) == d))(z_send(way, 0, PIECES).start)
+            for e in range(1, d):
+                pass_on(way, e, PIECES, upstream(way) == d - 1)
         if d == 1:
             for s in range(SLICES):
                 x_recv(1, s).wait_recv()
             add_base(sibling)
             add_base(across)
+            prompt_copy.wait_recv()
+            name_adapters(1)
         if d == 2:
             for s in range(SLICES):
                 x_recv(2, s).wait_recv()
             add_base(diagonal)
-        if d >= 2:
-            for way in range(2):
-                finish(way, d - 1)
-    for way in range(2):
-        pl.when(has_next(way))(z_send(way, 0, PIECES).start)
-    for way in range(2):
-        finish(way, peers - 1)
-
-    low_all[m] = low_sum[...].astype(jnp.bfloat16)
-    for i in range(3):
-        low_copy(i, None).start()
+        for way in range(2):
+            add_held(0, way, d)
+    for s in range(SLICES):
+        t_copy(s).wait_recv()
+    add_low(1, z, first=True)
     for d in range(1, peers):
         for way in range(2):
-            pass_on(way, d, PIECES)
-    for i, b in enumerate((across, sibling, diagonal)):
-        low_copy(i, b).wait_recv()
-    local[3].wait()
-    low = low_all[0].astype(jnp.float32)
-    for b in range(1, 4):
-        low += low_all[b].astype(jnp.float32)
-    low = low.astype(jnp.bfloat16)
+            add_held(1, way, d)
+
+    low_sent[...] = low_sum[...].astype(jnp.bfloat16)
+    for i in range(7):
+        low_copy(i).start()
+    low_all[g, m] = low_sent[0]
+    for way in range(2):
+        for e in range(1, peers):
+            pass_on(way, e, PIECES, upstream(way) == peers - 1)
+    for i in range(7):
+        low_recv(i).wait_recv()
+    lows = []
+    for side in range(2):
+        low = low_all[side, 0].astype(jnp.float32)
+        for b in range(1, 4):
+            low += low_all[side, b].astype(jnp.float32)
+        lows.append(low.astype(jnp.bfloat16))
+    low = jnp.concatenate(lows, axis=1)
+    local[6].wait()
     for d in range(1, peers):
         for way in range(2):
-            pl.when(has(way, d))(y_copy(way, d, PIECES, 1 - g).wait_recv)
-    for part in range(2):
-        spread = jnp.dot(low, fold(part, True), preferred_element_type=jnp.float32)
-        term = jnp.zeros((half, cols), jnp.float32)
+            pl.when(has(way, d))(y_copy(way, d, 1 - g).wait_recv)
+    for part in range(packed):
+
+        def spread_at(i, j, part=part):
+            inner = lax.rem(j, rank)
+            side = inner // part_rank
+            return i == side * (2 * rank) + part * part_rank + inner - side * part_rank
+
+        spread = jnp.dot(
+            low, ones((4 * rank, held * rank), spread_at), preferred_element_type=jnp.float32
+        )
+        term = jnp.zeros((quarter, cols), jnp.float32)
         for h in range(peers):
-            kept = jnp.where(member(h, part), spread, 0.0).astype(jnp.bfloat16)
+            kept = jnp.where(member(0, h, part, rank), spread, 0.0).astype(jnp.bfloat16)
             term += jnp.dot(kept, up_all[h], preferred_element_type=jnp.float32)
         term = term.astype(jnp.bfloat16).astype(jnp.float32)
-        here = pl.ds(part * half, half)
+        here = pl.ds(part * quarter, quarter)
         out[here, :] = (base[here, :] + 0.5 * term).astype(jnp.bfloat16)
 
+    prompt_copy.wait_send()
+    for s in range(SLICES):
+        t_copy(s).wait_send()
     for s in range(SLICES):
         for kind in range(3):
             x_copy(kind, s).wait_send()
-    for i in range(3):
-        low_copy(i, None).wait_send()
+    for i in range(7):
+        low_copy(i).wait_send()
     for way in range(2):
         for c in range(PIECES + 1):
             for d in range(peers - 1):
                 sent = has_next(way) if d == 0 else has_next(way) & has(way, d)
                 pl.when(sent)(z_send(way, d, c).wait_send)
-            for d in range(1, peers):
-                pl.when(has(way, d))(y_copy(way, d, c, g).wait_send)
+        for d in range(1, peers):
+            pl.when(has(way, d))(y_copy(way, d, g).wait_send)
 
 
 def grouped_update(token_rows, slot_ids, down_factor_sets, up_sets, reduce_fn):
@@ -444,38 +524,47 @@
     peers, mp = mesh.shape["req"], mesh.shape["mp"]
     rows, feats = tokens.shape
     held, rank, cols = up.shape
-    down_rows = jnp.transpose(down, (1, 2, 0)).reshape(held * rank, feats)
+    prompts = lengths.shape[1]
+    down_rows = jnp.transpose(down, (1, 2, 0))
     up_rows = up.reshape(held * rank, cols)
-    anywhere = pl.BlockSpec(memory_space=pl.ANY)
+    anywhere = pl.BlockSpec(memory_space=pltpu.HBM)
     vmem = pl.BlockSpec(memory_space=pltpu.VMEM)
     dma = pltpu.SemaphoreType.DMA
     hops = max(peers - 1, 1)
     return pl.pallas_call(
         functools.partial(adapter_kernel, peers, held, rank),
         out_shape=jax.ShapeDtypeStruct((rows, cols), jnp.bfloat16),
-        in_specs=[anywhere, vmem, vmem, vmem, anywhere, anywhere, anywhere],
+        in_specs=[anywhere] * 7,
         out_specs=vmem,
         scratch_shapes=[
             pltpu.VMEM((mp, rows, feats), jnp.bfloat16),
+            pltpu.VMEM((rows, feats), jnp.bfloat16),
             pltpu.VMEM(value_weight.shape, jnp.bfloat16),
-            pltpu.VMEM((peers, held * rank, feats), jnp.bfloat16),
+            pltpu.VMEM((peers, held, rank // 2, feats), jnp.bfloat16),
             pltpu.VMEM((peers, held * rank, cols), jnp.bfloat16),
-            pltpu.VMEM((mp, rows // 2, 2 * rank), jnp.bfloat16),
+            pltpu.VMEM((2, mp, rows // 4, 2 * rank), jnp.bfloat16),
+            pltpu.VMEM((2, rows // 4, 2 * rank), jnp.bfloat16),
             pltpu.VMEM((rows, cols), jnp.float32),
-            pltpu.VMEM((rows // 2, 2 * rank), jnp.float32),
-            pltpu.VMEM((rows, 1), jnp.int32),
-            dma((4,)),
+            pltpu.VMEM((2, rows // 4, 2 * rank), jnp.float32),
+            pltpu.VMEM((3, 1, prompts), jnp.int32),
+            pltpu.VMEM((2, 8, prompts), jnp.int32),
+            pltpu.VMEM((2, rows, 1), jnp.int32),
+            dma((7,)),
+            dma((1,)),
+            dma((1,)),
+            dma((SLICES,)),
+            dma((SLICES,)),
             dma((2, hops, PIECES + 1)),
             dma((2, hops, PIECES + 1)),
-            dma((2, hops, PIECES + 1)),
-            dma((2, hops, PIECES + 1)),
+            dma((2, hops)),
+            dma((2, hops)),
             dma((3, SLICES)),
             dma((3, SLICES)),
-            dma((3,)),
-            dma((3,)),
+            dma((7,)),
+            dma((7,)),
         ],
         compiler_params=pltpu.CompilerParams(
-            collective_id=0, has_side_effects=True, vmem_limit_bytes=48 << 20
+            collective_id=0, has_side_effects=True, vmem_limit_bytes=63 << 20
         ),
         cost_estimate=pl.CostEstimate(
             flops=2 * rows * feats * (mp * cols + peers * held * rank),

time: 59.2 us -> 49.1 us (0.83)
  local copies, waits for them, and re-layouts: 7.37 us -> 1.62 us
  Pallas kernels: 51.5 us -> 47.3 us
    unnamed x15 -> x1, local copies, waits for them, and re-layouts: 7.37 us -> 1.62 us
    pallas_call x1, Pallas kernels: 51.5 us -> 47.3 us  [gather_body(): pl.pallas_call(functools.partial(adapter_kernel, peers, held, rank), out_...]
where the time goes in v2:
time: 49.1 us; the launch traced here: 48.9 us
  Pallas kernels  47.3 us (96%)
  local copies, waits for them, and re-layouts  1.62 us (3%)
    pallas_call x1, Pallas kernels, gather_body(): pl.pallas_call(functools.partial(adapter_kernel, peers, held, rank), out_...  47.3 us
    unnamed x1, local copies, waits for them, and re-layouts  1.62 us

profile of v2, /device:TPU:0, one launch (start us, length us, event | category | flops | bytes accessed | tf_op | source)
XLA Modules:
  0.0 48.9 jit_solution(9409671551224534784)
XLA Ops:
  0.0 47.3 %shard_map.73 = bf16[384,256]{1,0:T(8,128)(2,1)} custom-call(bf16[384,1024]{1,0:T(8,128)(2,1)} %tok.1, s32[1,128]{1,0:T(1,128)} %lengths.1, s32[1,128]{1,0:T(1,128)} %bitcast.6, s32[1,128]{1,0:T(1,128)} %bitcast.7, bf16[4096,256]{1,0:T(8,128)(2,1)} %weight.1, bf16[5,64,1024]{2,1,0:T(8,128)(2,1)} %bitcast.4, bf16[320,256]{1,0:T(8,128)(2,1)} %bitcast.5), custom_call_target="tpu_custom_call" | custom-call | flops 1811939328 | bytes 3702784 | tf_op jit(solution)/shard_map/pallas_call | solution.py:534
  47.3 1.6 %copy.9 = bf16[384,256]{1,0:T(8,128)(2,1)} copy(bf16[384,256]{1,0:T(8,128)(2,1)} %shard_map.73) | data formatting | bytes 393216

commit v3 on v2

--- a/solution.py
+++ b/solution.py
@@ -35,6 +35,10 @@
     up_all,
     low_all,
     low_sent,
+    low_full,
+    low_back,
+    tok_end,
+    prompts_end,
     base,
     low_sum,
     small,
@@ -53,14 +57,21 @@
     x_recv_sem,
     low_send_sem,
     low_recv_sem,
+    full_send_sem,
+    full_recv_sem,
+    end_send_sem,
+    end_recv_sem,
+    back_send_sem,
+    back_recv_sem,
 ):
     rows, feats = tok.shape
     cols = out.shape[1]
-    part_rank = rank // 2
-    packed = 2 * rank // part_rank
-    width = held * part_rank
-    quarter = rows // packed
-    piece = feats // PIECES
+    width = held * rank
+    half = rows // 2
+    share = half // 4
+    mine = feats // 2
+    helped = mine // 2
+    piece = mine // PIECES
     batch = rows // SLICES
     g, z, m = lax.axis_index("groups"), lax.axis_index("req"), lax.axis_index("mp")
     sibling = m + 1 - 2 * lax.rem(m, 2)
@@ -79,30 +90,43 @@
 
     def strip(h, side, c):
         if c < PIECES:
-            return down_all.at[h, :, :, pl.ds(c * piece, piece)]
+            return down_all.at[h, :, pl.ds(c * piece, piece)]
         lanes = pl.ds(pl.multiple_of(side * (cols // 2), 128), cols // 2)
         return up_all.at[h, :, lanes]
 
-    def ranks_of(side):
-        return pl.ds(pl.multiple_of(side * part_rank, 16), part_rank)
+    def features(side, start, count):
+        return pl.ds(pl.multiple_of(side * mine + start, 128), count)
 
     def own_strip(c):
         if c < PIECES:
-            return down.at[:, ranks_of(g), pl.ds(c * piece, piece)]
+            return down.at[:, features(g, c * piece, piece)]
         lanes = pl.ds(pl.multiple_of(g * (cols // 2), 128), cols // 2)
         return up.at[:, lanes]
 
+    def inner(at):
+        return (at >= 1) & (at <= peers - 2)
+
+    is_end = (z == 0) | (z == peers - 1)
+    is_helper = (z == 1) | (z == peers - 2)
+    inward = 1 - 2 * lax.div(z, peers - 1)
+    outward = 2 * lax.div(z, 2) - 1
+
+    def helped_piece(c):
+        return c * piece < helped and c < PIECES
+
     def step_of(way):
         return 1 if way == 0 else -1
 
-    def has(way, d):
-        return z >= d if way == 0 else z + d <= peers - 1
+    def has(way, d, c=PIECES):
+        held_here = z >= d if way == 0 else z + d <= peers - 1
+        return held_here & inner(z) if helped_piece(c) else held_here
 
     def upstream(way):
         return z if way == 0 else peers - 1 - z
 
-    def has_next(way):
-        return z + 1 <= peers - 1 if way == 0 else z >= 1
+    def has_next(way, c=PIECES):
+        there = z + 1 <= peers - 1 if way == 0 else z >= 1
+        return there & inner(z + step_of(way)) if helped_piece(c) else there
 
     def z_send(way, d, c):
         h = z - step_of(way) * d
@@ -136,13 +160,48 @@
         )
 
     def t_copy(s):
-        there = pl.ds(s * batch, batch)
-        return remote(
-            tok.at[there],
-            tok_other.at[there],
+        return remote(
+            tok.at[:, features(1 - g, s * helped, helped)],
+            tok_other.at[:, pl.ds(s * helped, helped)],
             t_send_sem.at[s],
             t_recv_sem.at[s],
             {"groups": 1 - g},
+        )
+
+    def end_copy(i):
+        sources = (
+            tok.at[:, features(g, 0, helped)],
+            tok_other.at[:, pl.ds(0, helped)],
+            prompts_of,
+        )
+        targets = (tok_end.at[0], tok_end.at[1], prompts_end)
+        return remote(
+            sources[i],
+            targets[i],
+            end_send_sem.at[i],
+            end_recv_sem.at[i],
+            {"req": z + inward},
+        )
+
+    def end_recv(i):
+        target = (tok_end.at[0], tok_end.at[1], prompts_end)[i]
+        return remote(
+            target, target, end_send_sem.at[i], end_recv_sem.at[i], {"req": z + outward}
+        )
+
+    def back_copy(i):
+        return remote(
+            low_back.at[0, i],
+            low_back.at[1, i],
+            back_send_sem.at[i],
+            back_recv_sem.at[i],
+            {"req": z + outward},
+        )
+
+    def back_recv(i):
+        target = low_back.at[1, i]
+        return remote(
+            target, target, back_send_sem.at[i], back_recv_sem.at[i], {"req": z + inward}
         )
 
     def pass_on(way, d, c, when):
@@ -150,7 +209,7 @@
         def _():
             z_recv(way, d, c).wait_recv()
             if d < peers - 1:
-                pl.when(has_next(way))(z_send(way, d, c).start)
+                pl.when(has_next(way, c))(z_send(way, d, c).start)
             if c == PIECES:
                 y_copy(way, d, g).start()
 
@@ -183,9 +242,12 @@
     others = (across, sibling, diagonal)
     low_device = [{"mp": b} for b in others] + [{"groups": 1 - g, "mp": b} for b in others + (m,)]
 
+    def share_of(b):
+        return pl.ds(pl.multiple_of(b * share, 16), share)
+
     def low_copy(i):
         return remote(
-            low_sent.at[0 if i < 3 else 1],
+            low_sent.at[0 if i < 3 else 1, share_of((others + others + (m,))[i])],
             low_all.at[g, m],
             low_send_sem.at[i],
             low_recv_sem.at[i],
@@ -195,13 +257,21 @@
     def low_recv(i):
         target = low_all.at[g if i < 3 else 1 - g, (others + others + (m,))[i]]
         return remote(target, target, low_send_sem.at[i], low_recv_sem.at[i], low_device[i])
+
+    def full_copy(i):
+        here = low_full.at[share_of(m)]
+        return remote(here, here, full_send_sem.at[i], full_recv_sem.at[i], low_device[i])
+
+    def full_recv(i):
+        target = low_full.at[share_of(others[i])]
+        return remote(target, target, full_send_sem.at[i], full_recv_sem.at[i], low_device[i])
 
     local = [
         pltpu.make_async_copy(lengths, small.at[0], local_sem.at[0]),
         pltpu.make_async_copy(holder, small.at[1], local_sem.at[1]),
         pltpu.make_async_copy(place, small.at[2], local_sem.at[2]),
         pltpu.make_async_copy(tok, tok_all.at[m], local_sem.at[3]),
-        pltpu.make_async_copy(down.at[:, ranks_of(g)], down_all.at[z], local_sem.at[4]),
+        pltpu.make_async_copy(down.at[:, features(g, 0, mine)], down_all.at[z], local_sem.at[4]),
         pltpu.make_async_copy(weight, weight_here, local_sem.at[5]),
         pltpu.make_async_copy(up, up_all.at[z], local_sem.at[6]),
     ]
@@ -230,9 +300,10 @@
     beside = lax.div(z + peers - 1, peers) + lax.div(2 * peers - 2 - z, peers)
     pl.semaphore_wait(barrier, 7 + beside)
 
+    pl.when(is_end)(end_copy(0).start)
     for c in range(PIECES):
         for way in range(2):
-            pl.when(has_next(way))(z_send(way, 0, c).start)
+            pl.when(has_next(way, c))(z_send(way, 0, c).start)
     for way in range(2):
         pl.when(has_next(way) & (upstream(way) == 0))(z_send(way, 0, PIECES).start)
     prompt_copy = remote(
@@ -245,13 +316,14 @@
     prompt_copy.start()
     for s in range(SLICES):
         x_copy(0, s).start()
-    for s in range(SLICES):
+    for s in range(2):
         t_copy(s).start()
     for s in range(SLICES):
         x_copy(1, s).start()
 
     def name_adapters(which):
-        lens = prompts_of[which, 0:1]
+        table = prompts_of if which < 2 else prompts_end
+        lens = table[which % 2, 0:1]
         earlier = lax.broadcasted_iota(jnp.int32, (prompts, prompts), 0) <= lax.broadcasted_iota(
             jnp.int32, (prompts, prompts), 1
         )
@@ -262,7 +334,7 @@
         )[0:1].astype(jnp.int32)
         position = lax.broadcasted_iota(jnp.int32, (rows, prompts), 0)
         inside = (position < ends) & (position >= ends - lens)
-        named = jnp.where(inside, prompts_of[which, 1:2], 0)
+        named = jnp.where(inside, table[which % 2, 1:2], 0)
         adapter_of[which] = jnp.sum(named, axis=1, keepdims=True)
 
     name_adapters(0)
@@ -278,119 +350,149 @@
         else:
             base[...] += term
 
-    def member(which, h, part, per):
-        lane = lax.broadcasted_iota(jnp.int32, (1, held * per), 1)
-        owned = adapter_of[which, part * quarter : (part + 1) * quarter, :]
-        return owned == lane // per + h * held
-
-    def ones(shape, test):
-        one, two = (lax.broadcasted_iota(jnp.int32, shape, axis) for axis in range(2))
-        return test(one, two).astype(jnp.float32).astype(jnp.bfloat16)
-
-    def add_low(which, h, first=False):
+    def member(which, h, part):
+        lane = lax.broadcasted_iota(jnp.int32, (1, width), 1)
+        return adapter_of[which, part * half : (part + 1) * half, :] == lane // rank + h * held
+
+    def fold(part, turned):
+        shape = (2 * rank, width) if turned else (width, 2 * rank)
+        one = lax.broadcasted_iota(jnp.int32, shape, 1 if turned else 0)
+        two = lax.broadcasted_iota(jnp.int32, shape, 0 if turned else 1)
+        return (lax.rem(one, rank) == two - part * rank).astype(jnp.float32).astype(jnp.bfloat16)
+
+    def add_low(which, h, start, count, first=False):
+        if which == 0:
+            features_here = tok_all[m, :, features(g, start, count)]
+        elif which == 1:
+            features_here = tok_other[:, start : start + count]
+        else:
+            features_here = tok_end[which - 2]
         partial = lax.dot_general(
-            tok_all[m] if which == 0 else tok_other[...],
-            down_all[h].reshape(width, feats),
+            features_here,
+            down_all[h, :, start : start + count],
             (((1,), (1,)), ((), ())),
             preferred_element_type=jnp.float32,
         )
-        total = jnp.zeros((quarter, 2 * rank), jnp.float32)
-        for part in range(packed):
-            mine = partial[part * quarter : (part + 1) * quarter]
-            kept = jnp.where(member(which, h, part, part_rank), mine, 0.0).astype(jnp.bfloat16)
-            place_in = ones(
-                (width, 2 * rank),
-                lambda j, i: lax.rem(j, part_rank) == i - part * part_rank,
-            )
-            total += jnp.dot(kept, place_in, preferred_element_type=jnp.float32)
+        total = jnp.zeros((half, 2 * rank), jnp.float32)
+        for part in range(2):
+            ours = partial[part * half : (part + 1) * half]
+            kept = jnp.where(member(which, h, part), ours, 0.0).astype(jnp.bfloat16)
+            total += jnp.dot(kept, fold(part, False), preferred_element_type=jnp.float32)
         if first:
             low_sum[which] = total
         else:
             low_sum[which] += total
 
     def add_held(which, way, d):
-        @pl.when(has(way, d))
+        h = z - step_of(way) * d
+        pl.when(has(way, d) & inner(z))(lambda: add_low(which, h, 0, mine))
+        pl.when(has(way, d) & is_end)(lambda: add_low(which, h, helped, helped))
+
+    def help_end(i):
+        @pl.when(is_helper)
         def _():
-            add_low(which, z - step_of(way) * d)
+            end_recv(i).wait_recv()
+            if i == 0:
+                end_recv(2).wait_recv()
+            name_adapters(2 + i)
+            add_low(2 + i, z, 0, helped, first=True)
+            for d in range(1, peers - 1):
+                add_low(2 + i, z - outward * d, 0, helped)
+            low_back[0, i] = low_sum[2 + i].astype(jnp.bfloat16)
+            back_copy(i).start()
 
     local[3].wait()
     local[4].wait()
-    add_low(0, z, first=True)
+    add_low(0, z, 0, mine, first=True)
     local[5].wait()
     add_base(m, first=True)
+    x_slots = {2: 0, 5: 1, 8: 2, 11: 3}
     slot = 0
     for d in range(1, peers):
+        for way in range(2):
+            for e in range(1, d):
+                pass_on(way, e, PIECES, upstream(way) == d - 1)
+        if d == peers - 1:
+            help_end(0)
+            help_end(1)
         for c in range(PIECES):
             for way in range(2):
-                pass_on(way, d, c, has(way, d))
-            if slot < SLICES:
-                x_recv(0, slot).wait_recv()
-                x_copy(2, slot).start()
+                pass_on(way, d, c, has(way, d, c))
+            if slot in x_slots:
+                x_recv(0, x_slots[slot]).wait_recv()
+                x_copy(2, x_slots[slot]).start()
+            if slot == 1:
+                prompt_copy.wait_recv()
+                t_copy(0).wait_recv()
+
+                @pl.when(is_end)
+                def _():
+                    end_copy(2).start()
+                    end_copy(1).start()
+
             slot += 1
         for way in range(2):
             pl.when(has_next(way) & (upstream(way) == d))(z_send(way, 0, PIECES).start)
-            for e in range(1, d):
-                pass_on(way, e, PIECES, upstream(way) == d - 1)
         if d == 1:
+            name_adapters(1)
+            t_copy(1).wait_recv()
+            add_low(1, z, 0, mine, first=True)
             for s in range(SLICES):
                 x_recv(1, s).wait_recv()
             add_base(sibling)
-            add_base(across)
-            prompt_copy.wait_recv()
-            name_adapters(1)
-        if d == 2:
-            for s in range(SLICES):
-                x_recv(2, s).wait_recv()
-            add_base(diagonal)
         for way in range(2):
-            add_held(0, way, d)
-    for s in range(SLICES):
-        t_copy(s).wait_recv()
-    add_low(1, z, first=True)
-    for d in range(1, peers):
-        for way in range(2):
-            add_held(1, way, d)
-
-    low_sent[...] = low_sum[...].astype(jnp.bfloat16)
+            for which in range(2):
+                add_held(which, way, d)
+
+    @pl.when(is_end)
+    def _():
+        for i in range(2):
+            back_recv(i).wait_recv()
+            low_sum[i] += low_back[1, i].astype(jnp.float32)
+
+    low_sent[...] = low_sum[0:2].astype(jnp.bfloat16)
     for i in range(7):
         low_copy(i).start()
-    low_all[g, m] = low_sent[0]
+    low_all[g, m] = low_sent[0, share_of(m)]
+    add_base(across)
     for way in range(2):
         for e in range(1, peers):
             pass_on(way, e, PIECES, upstream(way) == peers - 1)
     for i in range(7):
         low_recv(i).wait_recv()
-    lows = []
-    for side in range(2):
-        low = low_all[side, 0].astype(jnp.float32)
-        for b in range(1, 4):
-            low += low_all[side, b].astype(jnp.float32)
-        lows.append(low.astype(jnp.bfloat16))
-    low = jnp.concatenate(lows, axis=1)
+    low = low_all[0, 0].astype(jnp.float32)
+    for i in range(1, 8):
+        low += low_all[i // 4, i % 4].astype(jnp.float32)
+    low_full[share_of(m)] = low.astype(jnp.bfloat16)
+    for i in range(3):
+        full_copy(i).start()
+    for s in range(SLICES):
+        x_recv(2, s).wait_recv()
+    add_base(diagonal)
     local[6].wait()
     for d in range(1, peers):
         for way in range(2):
             pl.when(has(way, d))(y_copy(way, d, 1 - g).wait_recv)
-    for part in range(packed):
-
-        def spread_at(i, j, part=part):
-            inner = lax.rem(j, rank)
-            side = inner // part_rank
-            return i == side * (2 * rank) + part * part_rank + inner - side * part_rank
-
-        spread = jnp.dot(
-            low, ones((4 * rank, held * rank), spread_at), preferred_element_type=jnp.float32
-        )
-        term = jnp.zeros((quarter, cols), jnp.float32)
+    for i in range(3):
+        full_recv(i).wait_recv()
+    low = low_full[...]
+    for part in range(2):
+        spread = jnp.dot(low, fold(part, True), preferred_element_type=jnp.float32)
+        term = jnp.zeros((half, cols), jnp.float32)
         for h in range(peers):
-            kept = jnp.where(member(0, h, part, rank), spread, 0.0).astype(jnp.bfloat16)
+            kept = jnp.where(member(0, h, part), spread, 0.0).astype(jnp.bfloat16)
             term += jnp.dot(kept, up_all[h], preferred_element_type=jnp.float32)
         term = term.astype(jnp.bfloat16).astype(jnp.float32)
-        here = pl.ds(part * quarter, quarter)
+        here = pl.ds(part * half, half)
         out[here, :] = (base[here, :] + 0.5 * term).astype(jnp.bfloat16)
 
+    for i in range(3):
+        full_copy(i).wait_send()
+        pl.when(is_end)(end_copy(i).wait_send)
+    for i in range(2):
+        pl.when(is_helper)(back_copy(i).wait_send)
     prompt_copy.wait_send()
-    for s in range(SLICES):
+    for s in range(2):
         t_copy(s).wait_send()
     for s in range(SLICES):
         for kind in range(3):
@@ -400,7 +502,7 @@
     for way in range(2):
         for c in range(PIECES + 1):
             for d in range(peers - 1):
-                sent = has_next(way) if d == 0 else has_next(way) & has(way, d)
+                sent = has_next(way, c) if d == 0 else has_next(way, c) & has(way, d, c)
                 pl.when(sent)(z_send(way, d, c).wait_send)
         for d in range(1, peers):
             pl.when(has(way, d))(y_copy(way, d, g).wait_send)
@@ -525,7 +627,7 @@
     rows, feats = tokens.shape
     held, rank, cols = up.shape
     prompts = lengths.shape[1]
-    down_rows = jnp.transpose(down, (1, 2, 0))
+    down_rows = jnp.transpose(down, (1, 2, 0)).reshape(held * rank, feats)
     up_rows = up.reshape(held * rank, cols)
     anywhere = pl.BlockSpec(memory_space=pltpu.HBM)
     vmem = pl.BlockSpec(memory_space=pltpu.VMEM)
@@ -538,22 +640,26 @@
         out_specs=vmem,
         scratch_shapes=[
             pltpu.VMEM((mp, rows, feats), jnp.bfloat16),
-            pltpu.VMEM((rows, feats), jnp.bfloat16),
+            pltpu.VMEM((rows, feats // 2), jnp.bfloat16),
             pltpu.VMEM(value_weight.shape, jnp.bfloat16),
-            pltpu.VMEM((peers, held, rank // 2, feats), jnp.bfloat16),
+            pltpu.VMEM((peers, held * rank, feats // 2), jnp.bfloat16),
             pltpu.VMEM((peers, held * rank, cols), jnp.bfloat16),
-            pltpu.VMEM((2, mp, rows // 4, 2 * rank), jnp.bfloat16),
-            pltpu.VMEM((2, rows // 4, 2 * rank), jnp.bfloat16),
+            pltpu.VMEM((2, mp, rows // 8, 2 * rank), jnp.bfloat16),
+            pltpu.VMEM((2, rows // 2, 2 * rank), jnp.bfloat16),
+            pltpu.VMEM((rows // 2, 2 * rank), jnp.bfloat16),
+            pltpu.VMEM((2, 2, rows // 2, 2 * rank), jnp.bfloat16),
+            pltpu.VMEM((2, rows, feats // 4), jnp.bfloat16),
+            pltpu.VMEM((2, 8, prompts), jnp.int32),
             pltpu.VMEM((rows, cols), jnp.float32),
-            pltpu.VMEM((2, rows // 4, 2 * rank), jnp.float32),
+            pltpu.VMEM((4, rows // 2, 2 * rank), jnp.float32),
             pltpu.VMEM((3, 1, prompts), jnp.int32),
             pltpu.VMEM((2, 8, prompts), jnp.int32),
-            pltpu.VMEM((2, rows, 1), jnp.int32),
+            pltpu.VMEM((4, rows, 1), jnp.int32),
             dma((7,)),
             dma((1,)),
             dma((1,)),
-            dma((SLICES,)),
-            dma((SLICES,)),
+            dma((2,)),
+            dma((2,)),
             dma((2, hops, PIECES + 1)),
             dma((2, hops, PIECES + 1)),
             dma((2, hops)),
@@ -562,6 +668,12 @@
             dma((3, SLICES)),
             dma((7,)),
             dma((7,)),
+            dma((3,)),
+            dma((3,)),
+            dma((3,)),
+            dma((3,)),
+            dma((2,)),
+            dma((2,)),
         ],
         compiler_params=pltpu.CompilerParams(
             collective_id=0, has_side_effects=True, vmem_limit_bytes=63 << 20
@@ -596,7 +708,7 @@
     def whole(*args):
         peers = mesh.shape["req"]
         moved = 2 * (args[5].size // mesh.shape["mp"] + args[6].size // mesh.shape["mp"])
-        fits = moved <= GATHER_BYTES and peers > 1
+        fits = moved <= GATHER_BYTES and peers == 4
         if fits and mesh.shape["mp"] == 4 and mesh.shape["groups"] == 2:
             part = functools.partial(gather_body, mesh)
         else:

time: 49.1 us -> 45.3 us (0.923)
  Pallas kernels: 47.3 us -> 43.5 us
    pallas_call x1, Pallas kernels: 47.3 us -> 43.5 us  [gather_body(): pl.pallas_call(functools.partial(adapter_kernel, peers, held, rank), out_...]
where the time goes in v3:
time: 45.3 us; the launch traced here: 45.2 us
  Pallas kernels  43.5 us (96%)
  local copies, waits for them, and re-layouts  1.62 us (4%)
    pallas_call x1, Pallas kernels, gather_body(): pl.pallas_call(functools.partial(adapter_kernel, peers, held, rank), out_...  43.5 us
    unnamed x1, local copies, waits for them, and re-layouts  1.62 us

profile of v3, /device:TPU:0, one launch (start us, length us, event | category | flops | bytes accessed | tf_op | source)
XLA Modules:
  0.0 45.2 jit_solution(586468956860128254)
XLA Ops:
  0.0 43.5 %shard_map.73 = bf16[384,256]{1,0:T(8,128)(2,1)} custom-call(bf16[384,1024]{1,0:T(8,128)(2,1)} %tok.1, s32[1,128]{1,0:T(1,128)} %lengths.1, s32[1,128]{1,0:T(1,128)} %bitcast.8, s32[1,128]{1,0:T(1,128)} %bitcast.9, bf16[4096,256]{1,0:T(8,128)(2,1)} %weight.1, bf16[320,1024]{1,0:T(8,128)(2,1)} %bitcast.6, bf16[320,256]{1,0:T(8,128)(2,1)} %bitcast.7), custom_call_target="tpu_custom_call" | custom-call | flops 1811939328 | bytes 3702784 | tf_op jit(solution)/shard_map/pallas_call | solution.py:636
  43.6 1.6 %copy.9 = bf16[384,256]{1,0:T(8,128)(2,1)} copy(bf16[384,256]{1,0:T(8,128)(2,1)} %shard_map.73) | data formatting | bytes 393216

commit v4 on v3

--- a/solution.py
+++ b/solution.py
@@ -71,7 +71,8 @@
     share = half // 4
     mine = feats // 2
     helped = mine // 2
-    piece = mine // PIECES
+    batches = PIECES // 2
+    piece = width // batches
     batch = rows // SLICES
     g, z, m = lax.axis_index("groups"), lax.axis_index("req"), lax.axis_index("mp")
     sibling = m + 1 - 2 * lax.rem(m, 2)
@@ -90,18 +91,20 @@
 
     def strip(h, side, c):
         if c < PIECES:
-            return down_all.at[h, :, pl.ds(c * piece, piece)]
-        lanes = pl.ds(pl.multiple_of(side * (cols // 2), 128), cols // 2)
-        return up_all.at[h, :, lanes]
+            return down_all.at[h, c // batches, pl.ds((c % batches) * piece, piece)]
+        return up_all.at[h, up_rows(side)]
+
+    def up_rows(side):
+        return pl.ds(pl.multiple_of(side * (width // 2), 16), width // 2)
 
     def features(side, start, count):
         return pl.ds(pl.multiple_of(side * mine + start, 128), count)
 
     def own_strip(c):
         if c < PIECES:
-            return down.at[:, features(g, c * piece, piece)]
-        lanes = pl.ds(pl.multiple_of(g * (cols // 2), 128), cols // 2)
-        return up.at[:, lanes]
+            lanes = features(g, (c // batches) * helped, helped)
+            return down.at[pl.ds((c % batches) * piece, piece), lanes]
+        return up.at[up_rows(g)]
 
     def inner(at):
         return (at >= 1) & (at <= peers - 2)
@@ -112,7 +115,7 @@
     outward = 2 * lax.div(z, 2) - 1
 
     def helped_piece(c):
-        return c * piece < helped and c < PIECES
+        return batches <= c < PIECES
 
     def step_of(way):
         return 1 if way == 0 else -1
@@ -120,9 +123,6 @@
     def has(way, d, c=PIECES):
         held_here = z >= d if way == 0 else z + d <= peers - 1
         return held_here & inner(z) if helped_piece(c) else held_here
-
-    def upstream(way):
-        return z if way == 0 else peers - 1 - z
 
     def has_next(way, c=PIECES):
         there = z + 1 <= peers - 1 if way == 0 else z >= 1
@@ -162,7 +162,7 @@
     def t_copy(s):
         return remote(
             tok.at[:, features(1 - g, s * helped, helped)],
-            tok_other.at[:, pl.ds(s * helped, helped)],
+            tok_other.at[s],
             t_send_sem.at[s],
             t_recv_sem.at[s],
             {"groups": 1 - g},
@@ -170,8 +170,8 @@
 
     def end_copy(i):
         sources = (
-            tok.at[:, features(g, 0, helped)],
-            tok_other.at[:, pl.ds(0, helped)],
+            tok.at[:, features(g, helped, helped)],
+            tok_other.at[1],
             prompts_of,
         )
         targets = (tok_end.at[0], tok_end.at[1], prompts_end)
@@ -271,7 +271,10 @@
         pltpu.make_async_copy(holder, small.at[1], local_sem.at[1]),
         pltpu.make_async_copy(place, small.at[2], local_sem.at[2]),
         pltpu.make_async_copy(tok, tok_all.at[m], local_sem.at[3]),
-        pltpu.make_async_copy(down.at[:, features(g, 0, mine)], down_all.at[z], local_sem.at[4]),
+        pltpu.make_async_copy(down.at[:, features(g, 0, helped)], down_all.at[z, 0], local_sem.at[4]),
+        pltpu.make_async_copy(
+            down.at[:, features(g, helped, helped)], down_all.at[z, 1], local_sem.at[7]
+        ),
         pltpu.make_async_copy(weight, weight_here, local_sem.at[5]),
         pltpu.make_async_copy(up, up_all.at[z], local_sem.at[6]),
     ]
@@ -301,11 +304,10 @@
     pl.semaphore_wait(barrier, 7 + beside)
 
     pl.when(is_end)(end_copy(0).start)
-    for c in range(PIECES):
+    order = [*range(batches), PIECES, *range(batches, PIECES)]
+    for c in order:
         for way in range(2):
             pl.when(has_next(way, c))(z_send(way, 0, c).start)
-    for way in range(2):
-        pl.when(has_next(way) & (upstream(way) == 0))(z_send(way, 0, PIECES).start)
     prompt_copy = remote(
         prompts_of.at[0],
         prompts_of.at[1],
@@ -316,7 +318,7 @@
     prompt_copy.start()
     for s in range(SLICES):
         x_copy(0, s).start()
-    for s in range(2):
+    for s in (1, 0):
         t_copy(s).start()
     for s in range(SLICES):
         x_copy(1, s).start()
@@ -361,18 +363,20 @@
         return (lax.rem(one, rank) == two - part * rank).astype(jnp.float32).astype(jnp.bfloat16)
 
     def add_low(which, h, start, count, first=False):
-        if which == 0:
-            features_here = tok_all[m, :, features(g, start, count)]
-        elif which == 1:
-            features_here = tok_other[:, start : start + count]
-        else:
-            features_here = tok_end[which - 2]
-        partial = lax.dot_general(
-            features_here,
-            down_all[h, :, start : start + count],
-            (((1,), (1,)), ((), ())),
-            preferred_element_type=jnp.float32,
-        )
+        partial = jnp.zeros((rows, width), jnp.float32)
+        for i in range(start // helped, (start + count) // helped):
+            if which == 0:
+                features_here = tok_all[m, :, features(g, i * helped, helped)]
+            elif which == 1:
+                features_here = tok_other[i]
+            else:
+                features_here = tok_end[which - 2]
+            partial += lax.dot_general(
+                features_here,
+                down_all[h, i],
+                (((1,), (1,)), ((), ())),
+                preferred_element_type=jnp.float32,
+            )
         total = jnp.zeros((half, 2 * rank), jnp.float32)
         for part in range(2):
             ours = partial[part * half : (part + 1) * half]
@@ -386,44 +390,48 @@
     def add_held(which, way, d):
         h = z - step_of(way) * d
         pl.when(has(way, d) & inner(z))(lambda: add_low(which, h, 0, mine))
-        pl.when(has(way, d) & is_end)(lambda: add_low(which, h, helped, helped))
-
-    def help_end(i):
+        pl.when(has(way, d) & is_end)(lambda: add_low(which, h, 0, helped))
+
+    def help_first(i):
         @pl.when(is_helper)
         def _():
             end_recv(i).wait_recv()
             if i == 0:
                 end_recv(2).wait_recv()
             name_adapters(2 + i)
-            add_low(2 + i, z, 0, helped, first=True)
-            for d in range(1, peers - 1):
-                add_low(2 + i, z - outward * d, 0, helped)
+            add_low(2 + i, z, helped, helped, first=True)
+            for d in range(1, peers - 2):
+                add_low(2 + i, z - outward * d, helped, helped)
+
+    def help_last(i):
+        @pl.when(is_helper)
+        def _():
+            add_low(2 + i, z - outward * (peers - 2), helped, helped)
             low_back[0, i] = low_sum[2 + i].astype(jnp.bfloat16)
             back_copy(i).start()
 
     local[3].wait()
     local[4].wait()
+    local[5].wait()
     add_low(0, z, 0, mine, first=True)
-    local[5].wait()
+    local[6].wait()
     add_base(m, first=True)
     x_slots = {2: 0, 5: 1, 8: 2, 11: 3}
     slot = 0
     for d in range(1, peers):
-        for way in range(2):
-            for e in range(1, d):
-                pass_on(way, e, PIECES, upstream(way) == d - 1)
-        if d == peers - 1:
-            help_end(0)
-            help_end(1)
-        for c in range(PIECES):
+        for c in order:
+            if d == peers - 2 and c == batches:
+                help_first(1)
             for way in range(2):
                 pass_on(way, d, c, has(way, d, c))
+            if c == PIECES:
+                continue
             if slot in x_slots:
                 x_recv(0, x_slots[slot]).wait_recv()
                 x_copy(2, x_slots[slot]).start()
             if slot == 1:
                 prompt_copy.wait_recv()
-                t_copy(0).wait_recv()
+                t_copy(1).wait_recv()
 
                 @pl.when(is_end)
                 def _():
@@ -431,11 +439,14 @@
                     end_copy(1).start()
 
             slot += 1
-        for way in range(2):
-            pl.when(has_next(way) & (upstream(way) == d))(z_send(way, 0, PIECES).start)
+        if d == 1:
+            help_first(0)
+        if d == peers - 2:
+            help_last(0)
+            help_last(1)
         if d == 1:
             name_adapters(1)
-            t_copy(1).wait_recv()
+            t_copy(0).wait_recv()
             add_low(1, z, 0, mine, first=True)
             for s in range(SLICES):
                 x_recv(1, s).wait_recv()
@@ -455,9 +466,6 @@
         low_copy(i).start()
     low_all[g, m] = low_sent[0, share_of(m)]
     add_base(across)
-    for way in range(2):
-        for e in range(1, peers):
-            pass_on(way, e, PIECES, upstream(way) == peers - 1)
     for i in range(7):
         low_recv(i).wait_recv()
     low = low_all[0, 0].astype(jnp.float32)
@@ -469,7 +477,7 @@
     for s in range(SLICES):
         x_recv(2, s).wait_recv()
     add_base(diagonal)
-    local[6].wait()
+    local[7].wait()
     for d in range(1, peers):
         for way in range(2):
             pl.when(has(way, d))(y_copy(way, d, 1 - g).wait_recv)
@@ -640,9 +648,9 @@
         out_specs=vmem,
         scratch_shapes=[
             pltpu.VMEM((mp, rows, feats), jnp.bfloat16),
-            pltpu.VMEM((rows, feats // 2), jnp.bfloat16),
+            pltpu.VMEM((2, rows, feats // 4), jnp.bfloat16),
             pltpu.VMEM(value_weight.shape, jnp.bfloat16),
-            pltpu.VMEM((peers, held * rank, feats // 2), jnp.bfloat16),
+            pltpu.VMEM((peers, 2, held * rank, feats // 4), jnp.bfloat16),
             pltpu.VMEM((peers, held * rank, cols), jnp.bfloat16),
             pltpu.VMEM((2, mp, rows // 8, 2 * rank), jnp.bfloat16),
             pltpu.VMEM((2, rows // 2, 2 * rank), jnp.bfloat16),
@@ -655,7 +663,7 @@
             pltpu.VMEM((3, 1, prompts), jnp.int32),
             pltpu.VMEM((2, 8, prompts), jnp.int32),
             pltpu.VMEM((4, rows, 1), jnp.int32),
-            dma((7,)),
+            dma((8,)),
             dma((1,)),
             dma((1,)),
             dma((2,)),

time: 45.3 us -> 43.5 us (0.960)
  Pallas kernels: 43.5 us -> 41.7 us
    pallas_call x1, Pallas kernels: 43.5 us -> 41.7 us  [gather_body(): pl.pallas_call(functools.partial(adapter_kernel, peers, held, rank), out_...]
where the time goes in v4:
time: 43.5 us; the launch traced here: 43.3 us
  Pallas kernels  41.7 us (96%)
  local copies, waits for them, and re-layouts  1.62 us (4%)
    pallas_call x1, Pallas kernels, gather_body(): pl.pallas_call(functools.partial(adapter_kernel, peers, held, rank), out_...  41.7 us
    unnamed x1, local copies, waits for them, and re-layouts  1.62 us

profile of v4, /device:TPU:0, one launch (start us, length us, event | category | flops | bytes accessed | tf_op | source)
XLA Modules:
  0.0 43.3 jit_solution(1649057211213692587)
XLA Ops:
  0.0 41.7 %shard_map.73 = bf16[384,256]{1,0:T(8,128)(2,1)} custom-call(bf16[384,1024]{1,0:T(8,128)(2,1)} %tok.1, s32[1,128]{1,0:T(1,128)} %lengths.1, s32[1,128]{1,0:T(1,128)} %bitcast.8, s32[1,128]{1,0:T(1,128)} %bitcast.9, bf16[4096,256]{1,0:T(8,128)(2,1)} %weight.1, bf16[320,1024]{1,0:T(8,128)(2,1)} %bitcast.6, bf16[320,256]{1,0:T(8,128)(2,1)} %bitcast.7), custom_call_target="tpu_custom_call" | custom-call | flops 1811939328 | bytes 3702784 | tf_op jit(solution)/shard_map/pallas_call | solution.py:644
  41.7 1.6 %copy.9 = bf16[384,256]{1,0:T(8,128)(2,1)} copy(bf16[384,256]{1,0:T(8,128)(2,1)} %shard_map.73) | data formatting | bytes 393216
